TPU v7x, 128 devices: a whole 4x4x4 slice. The times are simulated.
128 devices in a mesh: seg: 4 (over x), sec: 32 (over z, y, core).
Axes of the slice: x: 4, y: 4, z: 4, core: 2. Of those that a mesh axis runs over, the one named last changes fastest.
Arguments:
- left_env: bfloat16 [4, 32, 13, 512, 512], P('seg', 'sec'), may hold values from -0.25 to 0.25
- right_env: bfloat16 [4, 32, 13, 512, 512], P('seg', 'sec'), may hold values from -0.25 to 0.25
- left_block: bfloat16 [4, 32, 512, 512], P('seg', 'sec'), may hold values from -8 to 8
- right_block: bfloat16 [4, 32, 512, 512], P('seg', 'sec'), may hold values from -0.25 to 0.25
- inv_sv: bfloat16 [4, 32, 512], P('seg', 'sec'), may hold values from 0.5 to 2
- precond: float32 [4, 32, 512, 512], P('seg', 'sec'), may hold values from 1 to 4
- sector_dims: int32 [4, 32, 2], P('seg', 'sec'), may hold values from 128 to 512, as said below
- channel_charge: int32 [13], replicated, may hold values from -1 to 1
Outputs:
- next_vector: bfloat16 [4, 32, 512, 512], P('seg', 'sec')
- last_image: float32 [4, 32, 512, 512], P('seg', 'sec')
- projected: float32 [4, 4, 4], P('seg')
Inputs may be any that keep to these rules, and one draw needn't show every extreme that they name: `sector_dims`: in every segment some sector has left bond dimension 512 and some sector has right bond dimension 512.
All inputs are finite; a program needn't handle non-finite values.
Results may differ from a plain program's by a relative error of at most 0.024.
Values may be sent and summed in bfloat16 or wider, within the bound.
No kernel may reach another device: no remote copies, remote signals or barrier semaphores. Data moves between devices by JAX's collectives and lax.ppermute only.
A program may use at most 64 MiB of HBM per device.

v0:
```python
import functools

import jax
import jax.numpy as jnp
from jax import lax
from jax.experimental import pallas as pl
from jax.experimental.pallas import tpu as pltpu
from jax.sharding import PartitionSpec as P

MATVECS = 4
EPS = 1e-06
ROWS = 64
ROW = 1
MIB = 1 << 20
BF16 = jnp.bfloat16
F32 = jnp.float32
HV, HA, HE, HX, AA, AE, EE, UU = 0, 4, 8, 12, 16, 17, 18, 19

VMEM = pl.BlockSpec(memory_space=pltpu.VMEM)
SMEM = pl.BlockSpec(memory_space=pltpu.SMEM)
HBM = pl.BlockSpec(memory_space=pltpu.HBM)


def env_copies(slot, channel, refs):
    l_hbm, r_hbm, l_buf, r_buf, sems = refs
    return (
        pltpu.make_async_copy(l_hbm.at[channel], l_buf.at[slot], sems.at[slot, 0]),
        pltpu.make_async_copy(r_hbm.at[channel], r_buf.at[slot], sems.at[slot, 1]),
    )


def apply_channels(picked, first, last, x_ref, t_ref, acc, l_ref, r_ref, arrived=None):
    def lefts(i, slot):
        w = picked[i] if arrived is None else arrived(i)
        t_ref[slot] = jnp.dot(l_ref[w], x_ref[...], preferred_element_type=F32).astype(BF16)
        return w

    def term(w, slot):
        return lax.dot_general(
            t_ref[slot], r_ref[w], (((1,), (1,)), ((), ())), preferred_element_type=F32
        )

    def pair(h, carry):
        one = lefts(first + 2 * h, 0)
        two = lefts(first + 2 * h + 1, 1)
        acc[...] += term(one, 0) + term(two, 1)
        return carry

    count = last - first
    lax.fori_loop(0, lax.div(count, 2), pair, 0)

    @pl.when(lax.rem(count, 2) == 1)
    def _():
        acc[...] += term(lefts(last - 1, 0), 0)


def prepare_kernel(charge, far, dims, lb, precond, lb_out, inverse, plan, sems):
    copies = [
        pltpu.make_async_copy(lb, lb_out, sems.at[0]),
        pltpu.make_async_copy(precond, inverse, sems.at[1]),
    ]
    for copy in copies:
        copy.start()
    channels = charge.shape[0]
    n = jnp.int32(0)
    ends = []
    for wanted in (far[0], -far[0], 0):

        def body(w, n):
            hit = charge[w] == wanted

            @pl.when(hit)
            def _():
                plan[n] = w

            return n + hit.astype(jnp.int32)

        n = lax.fori_loop(0, channels, body, n)
        ends.append(n)
    plan[channels] = ends[0]
    plan[channels + 1] = jnp.maximum(ends[0], ends[1] - ends[0])
    plan[channels + 2] = ends[1]
    plan[channels + 3] = dims[0]
    plan[channels + 4] = dims[1]
    for copy in copies:
        copy.wait()
    inverse[...] = 1.0 / inverse[...]


def bounds(plan):
    channels = plan.shape[0] - 5
    return plan[channels], plan[channels + 1], plan[channels + 2]


def mask_of(plan, rows, width, first=0):
    channels = plan.shape[0] - 5
    a = lax.broadcasted_iota(jnp.int32, (rows, width), 0) + first
    b = lax.broadcasted_iota(jnp.int32, (rows, width), 1)
    return (a < plan[channels + 3]) & (b < plan[channels + 4])


def fold(x):
    return jnp.sum(x.reshape(x.shape[0] // 8, 8, x.shape[1]), axis=0)


def lanes_of(values, lanes):
    lane = lax.broadcasted_iota(jnp.int32, (8, 128), 1)
    out = jnp.zeros((8, 128), F32)
    for value, at in zip(values, lanes):
        whole = jnp.sum(jnp.sum(value, axis=0, keepdims=True), axis=1, keepdims=True)
        out = jnp.where(lane == at, whole, out)
    return out


def first_kernel(
    plan, lb, nb, inv, l_hbm, r_hbm, x_ref, far_ref, near_part, uu_ref,
    t_ref, acc, l_buf, r_buf, sems,
):
    refs = (l_hbm, r_hbm, l_buf, r_buf, sems)
    n_far, head, _ = bounds(plan)

    def start(i, carry):
        for copy in env_copies(i, plan[i], refs):
            copy.start()
        return carry

    lax.fori_loop(0, head, start, 0)
    scaled = (lb[...].astype(F32) * inv[...].astype(F32)).astype(BF16)
    guess = jnp.dot(scaled, nb[...], preferred_element_type=F32)
    guess = jnp.where(mask_of(plan, *guess.shape), guess, 0.0)
    x_ref[...] = guess.astype(BF16)
    uu_ref[...] = lanes_of([fold(guess * guess)], [UU])

    def arrived(i):
        for copy in env_copies(i, plan[i], refs):
            copy.wait()
        return i

    acc[...] = jnp.zeros_like(acc)
    near_part[...] = jnp.zeros_like(near_part)
    apply_channels(plan, 0, n_far, x_ref, t_ref, acc, l_buf, r_buf, arrived)
    far_ref[...] = acc[...].astype(BF16)
    apply_channels(plan, n_far, head, x_ref, t_ref, near_part, l_buf, r_buf, arrived)


def at(red, lane):
    return red[0:1, lane : lane + 1]


def scales_of(reds):
    return [lax.rsqrt(at(reds[0], UU) + EPS)] + [jnp.ones((1, 1), F32)] * (len(reds) - 1)


def solve_step(reds):
    k = len(reds) - 1
    s = scales_of(reds)
    red = reds[k]
    steps = range(k + 1)
    gram = {}
    for i in steps:
        for j in range(i + 1):
            gram[i, j] = gram[j, i] = s[i] * s[j] * at(reds[i], HX + j)
    column = [s[j] * s[k] * at(red, HV + j) for j in steps]
    theta = column[k]
    d = [s[j] * s[k] * (at(red, HA + j) - theta * at(red, HE + j)) for j in steps]
    cc = s[k] * s[k] * (at(red, AA) - 2.0 * theta * at(red, AE) + theta * theta * at(red, EE))
    pp = cc
    for i in steps:
        pp = pp - 2.0 * d[i] * d[i]
        for j in steps:
            pp = pp + d[i] * d[j] * gram[i, j]
    norm = lax.rsqrt(jnp.maximum(pp, 0.0) + EPS)
    return column, norm * s[k], norm * s[k] * theta, [norm * d[j] * s[j] for j in steps]


def following(reds, image, inverse, basis, out):
    _, w_v, w_x, w = solve_step(reds)
    k = len(reds) - 1

    def body(block, carry):
        rows = pl.ds(block * ROWS, ROWS)
        xs = [b[rows, :].astype(F32) for b in basis]
        p = (image[rows, :] * w_v - xs[k] * w_x) * inverse[rows, :]
        for j in range(k + 1):
            p = p - xs[j] * w[j]
        out[rows, :] = p.astype(BF16)
        return carry

    lax.fori_loop(0, out.shape[0] // ROWS, body, 0)


def next_kernel(k, scale, *refs):
    plan, got = refs[:2]
    older = refs[2 : 1 + k]
    basis = refs[1 + k : 1 + 2 * k]
    image, inverse, l_ref, r_ref, x_ref, far_ref, near_part, red_ref, t_ref, acc = refs[1 + 2 * k :]
    n_far, head, _ = bounds(plan)
    red_ref[...] = summed(got, scale)
    reds = [r[...] for r in older] + [red_ref[...]]
    following(reds, image, inverse, basis, x_ref)
    acc[...] = jnp.zeros_like(acc)
    near_part[...] = jnp.zeros_like(near_part)
    apply_channels(plan, 0, n_far, x_ref, t_ref, acc, l_ref, r_ref)
    far_ref[...] = acc[...].astype(BF16)
    apply_channels(plan, n_far, head, x_ref, t_ref, near_part, l_ref, r_ref)


def summed(got, scale):
    return jnp.broadcast_to(jnp.sum(got[...], axis=0) * scale, (8, 128))


def last_kernel(scale, *refs):
    k = MATVECS
    got = refs[0]
    older = refs[1:k]
    basis = refs[k : 2 * k]
    image, inverse, x_hbm, image_hbm, projected, x_buf, sems = refs[2 * k :]
    out = pltpu.make_async_copy(image, image_hbm, sems.at[0])
    out.start()
    reds = [r[...] for r in older] + [summed(got, scale)]
    following(reds, image, inverse, basis, x_buf)
    new = pltpu.make_async_copy(x_buf, x_hbm, sems.at[1])
    new.start()
    row = lax.broadcasted_iota(jnp.int32, (MATVECS, MATVECS), 0)
    col = lax.broadcasted_iota(jnp.int32, (MATVECS, MATVECS), 1)
    table = jnp.zeros((MATVECS, MATVECS), F32)
    for step in range(MATVECS):
        column = solve_step(reds[: step + 1])[0]
        for j in range(step + 1):
            table = jnp.where((row == j) & (col == step), column[j], table)
    projected[...] = table
    new.wait()
    out.wait()


def near_kernel(plan, x, near_part, l_ref, r_ref, near_ref, t_ref, acc):
    _, head, split = bounds(plan)
    acc[...] = near_part[...]
    apply_channels(plan, head, split, x, t_ref, acc, l_ref, r_ref)
    near_ref[...] = acc[...].astype(BF16)


def stay_kernel(k, plan, *refs):
    basis = refs[: k + 1]
    inverse, l_ref, r_ref, stay_ref, dots_ref, t_ref = refs[k + 1 :]
    split = bounds(plan)[2]
    width = stay_ref.shape[1]
    stay_ref[...] = jnp.zeros_like(stay_ref)
    apply_channels(plan, split, l_ref.shape[0], basis[k], t_ref, stay_ref, l_ref, r_ref)

    def body(block, sums):
        rows = pl.ds(block * ROWS, ROWS)
        xs = [b[rows, :].astype(F32) for b in basis]
        e = xs[k] * inverse[rows, :]
        new = [x * e for x in xs] + [x * xs[k] for x in xs] + [e * e]
        return tuple(total + fold(x) for total, x in zip(sums, new))

    zero = tuple(jnp.zeros((8, width), F32) for _ in range(2 * k + 3))
    sums = lax.fori_loop(0, stay_ref.shape[0] // ROWS, body, zero)
    lanes = [HE + j for j in range(k + 1)] + [HX + j for j in range(k + 1)] + [EE]
    dots_ref[...] = lanes_of(sums, lanes)


def joined_kernel(stay, from_far, out):
    out[...] = stay[...] + from_far[...].astype(F32)


def image_kernel(k, plan, *refs):
    basis = refs[: k + 1]
    stay, from_near, inverse, dots = refs[k + 1 : k + 5]
    rest = refs[k + 5 :]
    if k == 0:
        guess_dots, image, out = rest
    else:
        image, out = rest
    width = stay.shape[1]

    def body(block, sums):
        rows = pl.ds(block * ROWS, ROWS)
        v = stay[rows, :] + from_near[rows, :].astype(F32)
        v = jnp.where(mask_of(plan, ROWS, width, block * ROWS), v, 0.0)
        image[rows, :] = v
        xs = [b[rows, :].astype(F32) for b in basis]
        d = inverse[rows, :]
        a = v * d
        e = xs[k] * d
        new = [x * v for x in xs] + [x * a for x in xs] + [a * a, a * e]
        return tuple(total + fold(x) for total, x in zip(sums, new))

    zero = tuple(jnp.zeros((8, width), F32) for _ in range(2 * k + 4))
    sums = lax.fori_loop(0, stay.shape[0] // ROWS, body, zero)
    lanes = [HV + j for j in range(k + 1)] + [HA + j for j in range(k + 1)] + [AA, AE]
    total = lanes_of(sums, lanes) + dots[...]
    if k == 0:
        total = total + guess_dots[...]
    out[...] = jnp.broadcast_to(total[None, : out.shape[1]], out.shape)


def call(kernel, args, specs, outs, out_specs, scratch, flops, limit):
    return pl.pallas_call(
        kernel,
        out_shape=[jax.ShapeDtypeStruct(*o) for o in outs],
        in_specs=specs,
        out_specs=out_specs,
        scratch_shapes=scratch,
        compiler_params=pltpu.CompilerParams(vmem_limit_bytes=limit * MIB),
        cost_estimate=pl.CostEstimate(
            flops=flops, bytes_accessed=4 * MIB + flops // 512, transcendentals=0
        ),
    )(*args)


def in_hbm(*arrays):
    return [pltpu.with_memory_space_constraint(x, pltpu.HBM) for x in arrays]


def swapped(block, pairs):
    return lax.ppermute(block, "sec", pairs)


def per_device(
    left_env, right_env, left_block, right_block, inv_sv, precond, sector_dims, channel_charge
):
    width = left_block.shape[-1]
    sectors = lax.axis_size("sec")
    segments = lax.axis_size("seg")
    channels = left_env.shape[2]
    scale = 1.0 / (sectors * width * width)
    lenv, renv = left_env[0, 0], right_env[0, 0]
    dims = sector_dims[0, 0]
    odd = lax.rem(lax.axis_index("sec"), 2)
    far = (2 * odd - 1).astype(jnp.int32).reshape(1)
    far_pairs = [(i, i + 1) for i in range(1, sectors - 1, 2)]
    far_pairs += [(j, i) for i, j in far_pairs]
    near_pairs = [(i, i + 1) for i in range(0, sectors, 2)]
    near_pairs += [(j, i) for i, j in near_pairs]
    route = [((i + 1) % segments, i) for i in range(segments)]
    nb, inv = lax.ppermute((right_block[0, 0], inv_sv[0]), "seg", route)

    square = (width, width)
    small = ((8, 128), F32)
    one = 4 * width**3 * channels // 3
    left, inverse, plan = call(
        prepare_kernel,
        (channel_charge, far, dims, *in_hbm(left_block[0, 0], precond[0, 0])),
        [SMEM] * 3 + [HBM] * 2,
        [(square, BF16), (square, F32), ((channels + 5,), jnp.int32)],
        [VMEM, VMEM, SMEM],
        [pltpu.SemaphoreType.DMA((2,))], MIB, 8,
    )
    scratch = [pltpu.VMEM((2, width, width), BF16), pltpu.VMEM(square, F32)]
    buffers = [pltpu.VMEM(lenv.shape, BF16)] * 2 + [pltpu.SemaphoreType.DMA((channels, 2))]
    basis, reds = [], []
    for k in range(MATVECS):
        outs = [(square, BF16), (square, BF16), (square, F32), small]
        if k == 0:
            x, to_far, near_part, guess_dots = call(
                first_kernel,
                (plan, left, nb, inv, *in_hbm(lenv, renv)),
                [SMEM] + [VMEM] * 3 + [HBM] * 2,
                outs, [VMEM] * 4, scratch + buffers, 20 * one, 24,
            )
        else:
            x, to_far, near_part, red = call(
                functools.partial(next_kernel, k, scale),
                (plan, got, *reds, *basis, image, inverse, lenv, renv),
                [SMEM] + [VMEM] * (2 * k + 4),
                outs, [VMEM] * 4, scratch, one, 16,
            )
            reds.append(red)
        basis.append(x)
        from_far = swapped(to_far, far_pairs)
        (to_near,) = call(
            near_kernel, (plan, x, near_part, lenv, renv), [SMEM] + [VMEM] * 4,
            [(square, BF16)], [VMEM], scratch, one, 16,
        )
        from_near = swapped(to_near, near_pairs)
        stay, dots = call(
            functools.partial(stay_kernel, k),
            (plan, *basis, inverse, lenv, renv),
            [SMEM] + [VMEM] * (k + 4),
            [(square, F32), small], [VMEM] * 2,
            scratch[:1], one, 16,
        )
        (stay,) = call(
            joined_kernel, (stay, from_far), [VMEM] * 2, [(square, F32)], [VMEM], [], MIB, 16
        )
        extra = (guess_dots,) if k == 0 else ()
        image, spread = call(
            functools.partial(image_kernel, k),
            (plan, *basis, stay, from_near, inverse, dots, *extra),
            [SMEM] + [VMEM] * (k + 5 + len(extra)),
            [(square, F32), ((sectors, ROW, 128), F32)], [VMEM] * 2,
            [], MIB, 16,
        )
        got = lax.all_to_all(spread, "sec", 0, 0)
    x, image, projected = call(
        functools.partial(last_kernel, scale),
        (got, *reds, *basis, image, inverse),
        [VMEM] * (2 * MATVECS + 2),
        [(square, BF16), (square, F32), ((MATVECS, MATVECS), F32)], [HBM, HBM, VMEM],
        [pltpu.VMEM(square, BF16), pltpu.SemaphoreType.DMA((2,))], MIB, 16,
    )
    return (x[None, None], image[None, None], projected[None])


def solution(mesh):
    in_specs = (
        P("seg", "sec", None, None, None),
        P("seg", "sec", None, None, None),
        P("seg", "sec", None, None),
        P("seg", "sec", None, None),
        P("seg", "sec", None),
        P("seg", "sec", None, None),
        P("seg", "sec", None),
        P(),
    )
    out_specs = (P("seg", "sec", None, None), P("seg", "sec", None, None), P("seg", None, None))
    return jax.shard_map(
        per_device, mesh=mesh, in_specs=in_specs, out_specs=out_specs, check_vma=False
    )
```

profile of v0, /device:TPU:7, one launch (start us, length us, event | category | flops | bytes accessed | tf_op | source)
XLA Modules:
  0.0 144.1 jit_solution(14375155894550466213)
XLA Ops:
  0.6 0.6 collective-permute-start
  1.5 0.7 copy-done.2
  2.2 0.7 copy-done.3
  2.8 2.5 %shard_map.103 = (bf16[512,512]{1,0:T(8,128)(2,1)S(1)}, f32[512,512]{1,0:T(8,128)S(1)}, s32[18]{0:T(128)S(1)}) custom-call(s32[13]{0:T(128)S(1)} %copy-done.2, s32[1]{0:T(128)} %bitcast.far, s32[2]{0:T(128)S(1)} %bitcast.35, bf16[512,512]{1,0:T(8,128)(2,1)} %bitcast.37, f32[512,512]{1,0:T(8,128)} %bitcast.36), custom_call_target="tpu_custom_call" | custom-call | flops 1048576 | bytes 4196352 | tf_op jit(solution)/shard_map/pallas_call | solution.py:300
  5.4 9.6 %collective-permute-done.1.inv = bf16[1,512]{1,0:T(2,128)(2,1)S(1)} collective-permute-done((bf16[1,512]{1,0:T(2,128)(2,1)}, bf16[1,512]{1,0:T(2,128)(2,1)S(1)}, u32[]{:S(2)}, u32[]{:S(2)}) %collective-permute-start.1) | collective-permute-done | bytes 1056 | tf_op jit(solution)/shard_map/ppermute | solution.py:338
  14.9 5.9 %shard_map.104 = (bf16[512,512]{1,0:T(8,128)(2,1)S(1)}, bf16[512,512]{1,0:T(8,128)(2,1)S(1)}, f32[512,512]{1,0:T(8,128)S(1)}, f32[8,128]{1,0:T(8,128)S(1)}) custom-call(s32[18]{0:T(128)S(1)} %get-tuple-element.41.plan.refs_0_, bf16[512,512]{1,0:T(8,128)(2,1)S(1)} %get-tuple-element.42.lb, bf16[512,512]{1,0:T(8,128)(2,1)S(1)} %collective-permute-done.nb, ...), custom_call_target="tpu_custom_call" | custom-call | flops 46528811008 | bytes 95070888 | tf_op jit(solution)/shard_map/pallas_call | solution.py:300
  20.8 4.7 %collective-permute-start.2 = (bf16[512,512]{1,0:T(8,128)(2,1)S(1)}, bf16[512,512]{1,0:T(8,128)(2,1)S(1)}, u32[]{:S(2)}, u32[]{:S(2)}) collective-permute-start(bf16[512,512]{1,0:T(8,128)(2,1)S(1)} %get-tuple-element.46), channel_id=1, source_target_pairs={{1,2},{3,4},{5,6},{7,8},{9,10},{11,12},{13,14},{15,16},{17,18},{19... | collective-permute-start | bytes 1572872 | tf_op jit(solution)/shard_map/ppermute | solution.py:318
  25.5 2.6 %shard_map.107 = bf16[512,512]{1,0:T(8,128)(2,1)S(1)} custom-call(s32[18]{0:T(128)S(1)} %get-tuple-element.41.plan.refs_0_, bf16[512,512]{1,0:T(8,128)(2,1)S(1)} %get-tuple-element.43.refs_0_.x.refs_2_.refs_3_.refs_4_, f32[512,512]{1,0:T(8,128)S(1)} %get-tuple-element.47.near_part, bf16[13,512,512]{2,1,0:T(8,128)(2,1)S(1)} %bitcast.12, ...), custom_call_target="tpu_custom_call" | custom-call | flops 2326440704 | bytes 8738133 | tf_op jit(solution)/shard_map/pallas_call | solution.py:300
  28.2 4.2 %shard_map.105 = (f32[512,512]{1,0:T(8,128)S(1)}, f32[8,128]{1,0:T(8,128)S(1)}) custom-call(s32[18]{0:T(128)S(1)} %get-tuple-element.41.plan.refs_0_, bf16[512,512]{1,0:T(8,128)(2,1)S(1)} %get-tuple-element.43.refs_0_.x.refs_2_.refs_3_.refs_4_, f32[512,512]{1,0:T(8,128)S(1)} %get-tuple-element.44.refs_1_.refs_3_.refs_4_.refs_2_.refs_6_.refs_5_.refs_8_.refs_9_, ...), custom_call_target="tpu_custom_call" | custom-call | flops 2326440704 | bytes 8738133 | tf_op jit(solution)/shard_map/pallas_call | solution.py:300
  32.6 1.3 shard_map.108
  33.9 15.6 %all_to_all.20.refs_1_ = f32[32,1,128]{2,1,0:T(1,128)S(1)} all-to-all(f32[32,1,128]{2,1,0:T(1,128)S(1)} %get-tuple-element.50), channel_id=1, replica_groups=mesh['seg'=4,'sec'=32] {'sec'}, dimensions={0} | all-to-all | bytes 32768 | tf_op jit(solution)/shard_map/all_to_all | solution.py:396
  49.5 5.4 %shard_map.109 = (bf16[512,512]{1,0:T(8,128)(2,1)S(1)}, bf16[512,512]{1,0:T(8,128)(2,1)S(1)}, f32[512,512]{1,0:T(8,128)S(1)}, f32[8,128]{1,0:T(8,128)S(1)}) custom-call(s32[18]{0:T(128)S(1)} %get-tuple-element.41.plan.refs_0_, f32[32,1,128]{2,1,0:T(1,128)S(1)} %all_to_all.20.refs_1_, ...), custom_call_target="tpu_custom_call" | custom-call | flops 2326440704 | bytes 8738133 | tf_op jit(solution)/shard_map/pallas_call | solution.py:300
  54.9 2.7 %collective-permute-start.4 = (bf16[512,512]{1,0:T(8,128)(2,1)S(1)}, bf16[512,512]{1,0:T(8,128)(2,1)S(1)}, u32[]{:S(2)}, u32[]{:S(2)}) collective-permute-start(bf16[512,512]{1,0:T(8,128)(2,1)S(1)} %get-tuple-element.54), channel_id=1, source_target_pairs={{1,2},{3,4},{5,6},{7,8},{9,10},{11,12},{13,14},{15,16},{17,18},{19... | collective-permute-start | bytes 1572872 | tf_op jit(solution)/shard_map/ppermute | solution.py:318
  57.6 2.6 %shard_map.112 = bf16[512,512]{1,0:T(8,128)(2,1)S(1)} custom-call(s32[18]{0:T(128)S(1)} %get-tuple-element.41.plan.refs_0_, bf16[512,512]{1,0:T(8,128)(2,1)S(1)} %get-tuple-element.52.refs_1_.x.refs_4_.refs_5_, f32[512,512]{1,0:T(8,128)S(1)} %get-tuple-element.55.near_part, bf16[13,512,512]{2,1,0:T(8,128)(2,1)S(1)} %bitcast.15, ...), custom_call_target="tpu_custom_call" | custom-call | flops 2326440704 | bytes 8738133 | tf_op jit(solution)/shard_map/pallas_call | solution.py:300
  60.5 4.4 %shard_map.110 = (f32[512,512]{1,0:T(8,128)S(1)}, f32[8,128]{1,0:T(8,128)S(1)}) custom-call(s32[18]{0:T(128)S(1)} %get-tuple-element.41.plan.refs_0_, bf16[512,512]{1,0:T(8,128)(2,1)S(1)} %get-tuple-element.43.refs_0_.x.refs_2_.refs_3_.refs_4_, bf16[512,512]{1,0:T(8,128)(2,1)S(1)} %get-tuple-element.52.refs_1_.x.refs_4_.refs_5_, ...), custom_call_target="tpu_custom_call" | custom-call | flops 2326440704 | bytes 8738133 | tf_op jit(solution)/shard_map/pallas_call | solution.py:300
  64.9 0.5 collective-permute-done.4.from_far
  65.5 1.5 %shard_map.113 = (f32[512,512]{1,0:T(8,128)S(1)}, f32[32,1,128]{2,1,0:T(1,128)S(1)}) custom-call(s32[18]{0:T(128)S(1)} %get-tuple-element.41.plan.refs_0_, bf16[512,512]{1,0:T(8,128)(2,1)S(1)} %get-tuple-element.43.refs_0_.x.refs_2_.refs_3_.refs_4_, bf16[512,512]{1,0:T(8,128)(2,1)S(1)} %get-tuple-element.52.refs_1_.x.refs_4_.refs_5_, ...), custom_call_target="tpu_custom_call" | custom-call | flops 1048576 | bytes 4196352 | tf_op jit(solution)/shard_map/pallas_call | solution.py:300
  67.0 12.4 %all_to_all.21.refs_1_ = f32[32,1,128]{2,1,0:T(1,128)S(1)} all-to-all(f32[32,1,128]{2,1,0:T(1,128)S(1)} %get-tuple-element.57), channel_id=1, replica_groups=mesh['seg'=4,'sec'=32] {'sec'}, dimensions={0} | all-to-all | bytes 32768 | tf_op jit(solution)/shard_map/all_to_all | solution.py:396
  79.3 5.5 %shard_map.114 = (bf16[512,512]{1,0:T(8,128)(2,1)S(1)}, bf16[512,512]{1,0:T(8,128)(2,1)S(1)}, f32[512,512]{1,0:T(8,128)S(1)}, f32[8,128]{1,0:T(8,128)S(1)}) custom-call(s32[18]{0:T(128)S(1)} %get-tuple-element.41.plan.refs_0_, f32[32,1,128]{2,1,0:T(1,128)S(1)} %all_to_all.21.refs_1_, f32[8,128]{1,0:T(8,128)S(1)} %get-tuple-element.58.refs_2_.refs_1_, ...), custom_call_target="tpu_custom_call" | custom-call | flops 2326440704 | bytes 8738133 | tf_op jit(solution)/shard_map/pallas_call | solution.py:300
  84.9 2.7 %collective-permute-start.6 = (bf16[512,512]{1,0:T(8,128)(2,1)S(1)}, bf16[512,512]{1,0:T(8,128)(2,1)S(1)}, u32[]{:S(2)}, u32[]{:S(2)}) collective-permute-start(bf16[512,512]{1,0:T(8,128)(2,1)S(1)} %get-tuple-element.62), channel_id=1, source_target_pairs={{1,2},{3,4},{5,6},{7,8},{9,10},{11,12},{13,14},{15,16},{17,18},{19... | collective-permute-start | bytes 1572872 | tf_op jit(solution)/shard_map/ppermute | solution.py:318
  87.6 2.6 %shard_map.117 = bf16[512,512]{1,0:T(8,128)(2,1)S(1)} custom-call(s32[18]{0:T(128)S(1)} %get-tuple-element.41.plan.refs_0_, bf16[512,512]{1,0:T(8,128)(2,1)S(1)} %get-tuple-element.60.refs_2_.x.refs_6_, f32[512,512]{1,0:T(8,128)S(1)} %get-tuple-element.63.near_part, bf16[13,512,512]{2,1,0:T(8,128)(2,1)S(1)} %bitcast.18, bf16[13,512,512]{2,1,0:T(8,128)(2,1)S(1)} %bitcast.30), custom_call_target="tpu_custom_call" | custom-call | flops 2326440704 | bytes 8738133 | tf_op jit(solution)/shard_map/pallas_call | solution.py:300
  90.4 4.5 %shard_map.115 = (f32[512,512]{1,0:T(8,128)S(1)}, f32[8,128]{1,0:T(8,128)S(1)}) custom-call(s32[18]{0:T(128)S(1)} %get-tuple-element.41.plan.refs_0_, bf16[512,512]{1,0:T(8,128)(2,1)S(1)} %get-tuple-element.43.refs_0_.x.refs_2_.refs_3_.refs_4_, bf16[512,512]{1,0:T(8,128)(2,1)S(1)} %get-tuple-element.52.refs_1_.x.refs_4_.refs_5_, ...), custom_call_target="tpu_custom_call" | custom-call | flops 2326440704 | bytes 8738133 | tf_op jit(solution)/shard_map/pallas_call | solution.py:300
  94.9 0.5 collective-permute-done.6.from_far
  95.5 1.7 %shard_map.118 = (f32[512,512]{1,0:T(8,128)S(1)}, f32[32,1,128]{2,1,0:T(1,128)S(1)}) custom-call(s32[18]{0:T(128)S(1)} %get-tuple-element.41.plan.refs_0_, bf16[512,512]{1,0:T(8,128)(2,1)S(1)} %get-tuple-element.43.refs_0_.x.refs_2_.refs_3_.refs_4_, bf16[512,512]{1,0:T(8,128)(2,1)S(1)} %get-tuple-element.52.refs_1_.x.refs_4_.refs_5_, ...), custom_call_target="tpu_custom_call" | custom-call | flops 1048576 | bytes 4196352 | tf_op jit(solution)/shard_map/pallas_call | solution.py:300
  97.3 12.3 %all_to_all.22.refs_1_ = f32[32,1,128]{2,1,0:T(1,128)S(1)} all-to-all(f32[32,1,128]{2,1,0:T(1,128)S(1)} %get-tuple-element.65), channel_id=1, replica_groups=mesh['seg'=4,'sec'=32] {'sec'}, dimensions={0} | all-to-all | bytes 32768 | tf_op jit(solution)/shard_map/all_to_all | solution.py:396
  109.6 5.6 %shard_map.119 = (bf16[512,512]{1,0:T(8,128)(2,1)S(1)}, bf16[512,512]{1,0:T(8,128)(2,1)S(1)}, f32[512,512]{1,0:T(8,128)S(1)}, f32[8,128]{1,0:T(8,128)S(1)}) custom-call(s32[18]{0:T(128)S(1)} %get-tuple-element.41.plan.refs_0_, f32[32,1,128]{2,1,0:T(1,128)S(1)} %all_to_all.22.refs_1_, f32[8,128]{1,0:T(8,128)S(1)} %get-tuple-element.58.refs_2_.refs_1_, ...), custom_call_target="tpu_custom_call" | custom-call | flops 2326440704 | bytes 8738133 | tf_op jit(solution)/shard_map/pallas_call | solution.py:300
  115.2 2.7 %collective-permute-start.8 = (bf16[512,512]{1,0:T(8,128)(2,1)S(1)}, bf16[512,512]{1,0:T(8,128)(2,1)S(1)}, u32[]{:S(2)}, u32[]{:S(2)}) collective-permute-start(bf16[512,512]{1,0:T(8,128)(2,1)S(1)} %get-tuple-element.70), channel_id=1, source_target_pairs={{1,2},{3,4},{5,6},{7,8},{9,10},{11,12},{13,14},{15,16},{17,18},{19... | collective-permute-start | bytes 1572872 | tf_op jit(solution)/shard_map/ppermute | solution.py:318
  118.0 2.8 %shard_map.122 = bf16[512,512]{1,0:T(8,128)(2,1)S(1)} custom-call(s32[18]{0:T(128)S(1)} %get-tuple-element.41.plan.refs_0_, bf16[512,512]{1,0:T(8,128)(2,1)S(1)} %get-tuple-element.68.refs_3_.x.refs_7_, f32[512,512]{1,0:T(8,128)S(1)} %get-tuple-element.71.near_part, bf16[13,512,512]{2,1,0:T(8,128)(2,1)S(1)} %bitcast.21, bf16[13,512,512]{2,1,0:T(8,128)(2,1)S(1)} %bitcast.33), custom_call_target="tpu_custom_call" | custom-call | flops 2326440704 | bytes 8738133 | tf_op jit(solution)/shard_map/pallas_call | solution.py:300
  121.0 4.7 %shard_map.120 = (f32[512,512]{1,0:T(8,128)S(1)}, f32[8,128]{1,0:T(8,128)S(1)}) custom-call(s32[18]{0:T(128)S(1)} %get-tuple-element.41.plan.refs_0_, bf16[512,512]{1,0:T(8,128)(2,1)S(1)} %get-tuple-element.43.refs_0_.x.refs_2_.refs_3_.refs_4_, bf16[512,512]{1,0:T(8,128)(2,1)S(1)} %get-tuple-element.52.refs_1_.x.refs_4_.refs_5_, ...), custom_call_target="tpu_custom_call" | custom-call | flops 2326440704 | bytes 8738133 | tf_op jit(solution)/shard_map/pallas_call | solution.py:300
  125.9 2.0 %shard_map.123 = (f32[512,512]{1,0:T(8,128)S(1)}, f32[32,1,128]{2,1,0:T(1,128)S(1)}) custom-call(s32[18]{0:T(128)S(1)} %get-tuple-element.41.plan.refs_0_, bf16[512,512]{1,0:T(8,128)(2,1)S(1)} %get-tuple-element.43.refs_0_.x.refs_2_.refs_3_.refs_4_, bf16[512,512]{1,0:T(8,128)(2,1)S(1)} %get-tuple-element.52.refs_1_.x.refs_4_.refs_5_, ...), custom_call_target="tpu_custom_call" | custom-call | flops 1048576 | bytes 4196352 | tf_op jit(solution)/shard_map/pallas_call | solution.py:300
  127.9 12.8 %all_to_all.23.refs_0_ = f32[32,1,128]{2,1,0:T(1,128)S(1)} all-to-all(f32[32,1,128]{2,1,0:T(1,128)S(1)} %get-tuple-element.73), channel_id=1, replica_groups=mesh['seg'=4,'sec'=32] {'sec'}, dimensions={0} | all-to-all | bytes 32768 | tf_op jit(solution)/shard_map/all_to_all | solution.py:396
  140.7 3.2 %shard_map.124 = (bf16[512,512]{1,0:T(8,128)(2,1)}, f32[512,512]{1,0:T(8,128)}, f32[4,4]{1,0:T(4,128)}) custom-call(f32[32,1,128]{2,1,0:T(1,128)S(1)} %all_to_all.23.refs_0_, f32[8,128]{1,0:T(8,128)S(1)} %get-tuple-element.58.refs_2_.refs_1_, f32[8,128]{1,0:T(8,128)S(1)} %get-tuple-element.66.refs_3_.refs_2_, f32[8,128]{1,0:T(8,128)S(1)} %get-tuple-element.74.refs_3_, ...), custom_call_target="tpu_custom_call" | custom-call | flops 1048576 | bytes 4196352 | tf_op jit(solution)/shard_map/pallas_call | solution.py:300
  (22 shorter events, 1.3 us)
Async XLA Ops:
  0.6 14.3 %collective-permute-start = (bf16[512,512]{1,0:T(8,128)(2,1)}, bf16[512,512]{1,0:T(8,128)(2,1)S(1)}, u32[]{:S(2)}, u32[]{:S(2)}) collective-permute-start(bf16[512,512]{1,0:T(8,128)(2,1)} %bitcast.39), channel_id=1, source_target_pairs={{32,0},{64,32},{96,64},{0,96},{33,1},{65,33},{97,65},{1,97},{34,2}... | collective-permute-start | bytes 1572872 | tf_op jit(solution)/shard_map/ppermute | solution.py:338
  1.2 13.7 %collective-permute-start.1 = (bf16[1,512]{1,0:T(2,128)(2,1)}, bf16[1,512]{1,0:T(2,128)(2,1)S(1)}, u32[]{:S(2)}, u32[]{:S(2)}) collective-permute-start(bf16[1,512]{1,0:T(2,128)(2,1)} %bitcast.41), channel_id=1, source_target_pairs={{32,0},{64,32},{96,64},{0,96},{33,1},{65,33},{97,65},{1,97},{34,2}... | collective-permute-start | bytes 3080 | tf_op jit(solution)/shard_map/ppermute | solution.py:338
  1.5 0.7 copy-start.2
  2.2 0.7 copy-start.3
  14.9 10.6 %copy-start = (bf16[1,1,13,512,512]{4,3,2,1,0:T(8,128)(2,1)S(1)}, bf16[1,1,13,512,512]{4,3,2,1,0:T(8,128)(2,1)}, u32[]{:S(2)}) copy-start(bf16[1,1,13,512,512]{4,3,2,1,0:T(8,128)(2,1)} %param.8) | copy-start | bytes 20447236
  14.9 10.6 %copy-start.1 = (bf16[1,1,13,512,512]{4,3,2,1,0:T(8,128)(2,1)S(1)}, bf16[1,1,13,512,512]{4,3,2,1,0:T(8,128)(2,1)}, u32[]{:S(2)}) copy-start(bf16[1,1,13,512,512]{4,3,2,1,0:T(8,128)(2,1)} %param.9) | copy-start | bytes 20447236
  20.8 11.6 %collective-permute-start.2 = (bf16[512,512]{1,0:T(8,128)(2,1)S(1)}, bf16[512,512]{1,0:T(8,128)(2,1)S(1)}, u32[]{:S(2)}, u32[]{:S(2)}) collective-permute-start(bf16[512,512]{1,0:T(8,128)(2,1)S(1)} %get-tuple-element.46), channel_id=1, source_target_pairs={{1,2},{3,4},{5,6},{7,8},{9,10},{11,12},{13,14},{15,16},{17,18},{19... | collective-permute-start | bytes 1572872 | tf_op jit(solution)/shard_map/ppermute | solution.py:318
  28.2 4.4 %collective-permute-start.3 = (bf16[512,512]{1,0:T(8,128)(2,1)S(1)}, bf16[512,512]{1,0:T(8,128)(2,1)S(1)}, u32[]{:S(2)}, u32[]{:S(2)}) collective-permute-start(bf16[512,512]{1,0:T(8,128)(2,1)S(1)} %shard_map.107), channel_id=1, source_target_pairs={{0,1},{2,3},{4,5},{6,7},{8,9},{10,11},{12,13},{14,15},{16,17},{18,... | collective-permute-start | bytes 1572872 | tf_op jit(solution)/shard_map/ppermute | solution.py:318
  54.9 10.5 %collective-permute-start.4 = (bf16[512,512]{1,0:T(8,128)(2,1)S(1)}, bf16[512,512]{1,0:T(8,128)(2,1)S(1)}, u32[]{:S(2)}, u32[]{:S(2)}) collective-permute-start(bf16[512,512]{1,0:T(8,128)(2,1)S(1)} %get-tuple-element.54), channel_id=1, source_target_pairs={{1,2},{3,4},{5,6},{7,8},{9,10},{11,12},{13,14},{15,16},{17,18},{19... | collective-permute-start | bytes 1572872 | tf_op jit(solution)/shard_map/ppermute | solution.py:318
  60.3 5.2 %collective-permute-start.5 = (bf16[512,512]{1,0:T(8,128)(2,1)S(1)}, bf16[512,512]{1,0:T(8,128)(2,1)S(1)}, u32[]{:S(2)}, u32[]{:S(2)}) collective-permute-start(bf16[512,512]{1,0:T(8,128)(2,1)S(1)} %shard_map.112), channel_id=1, source_target_pairs={{0,1},{2,3},{4,5},{6,7},{8,9},{10,11},{12,13},{14,15},{16,17},{18,... | collective-permute-start | bytes 1572872 | tf_op jit(solution)/shard_map/ppermute | solution.py:318
  84.9 10.5 %collective-permute-start.6 = (bf16[512,512]{1,0:T(8,128)(2,1)S(1)}, bf16[512,512]{1,0:T(8,128)(2,1)S(1)}, u32[]{:S(2)}, u32[]{:S(2)}) collective-permute-start(bf16[512,512]{1,0:T(8,128)(2,1)S(1)} %get-tuple-element.62), channel_id=1, source_target_pairs={{1,2},{3,4},{5,6},{7,8},{9,10},{11,12},{13,14},{15,16},{17,18},{19... | collective-permute-start | bytes 1572872 | tf_op jit(solution)/shard_map/ppermute | solution.py:318
  90.3 5.3 %collective-permute-start.7 = (bf16[512,512]{1,0:T(8,128)(2,1)S(1)}, bf16[512,512]{1,0:T(8,128)(2,1)S(1)}, u32[]{:S(2)}, u32[]{:S(2)}) collective-permute-start(bf16[512,512]{1,0:T(8,128)(2,1)S(1)} %shard_map.117), channel_id=1, source_target_pairs={{0,1},{2,3},{4,5},{6,7},{8,9},{10,11},{12,13},{14,15},{16,17},{18,... | collective-permute-start | bytes 1572872 | tf_op jit(solution)/shard_map/ppermute | solution.py:318
  115.2 10.5 %collective-permute-start.8 = (bf16[512,512]{1,0:T(8,128)(2,1)S(1)}, bf16[512,512]{1,0:T(8,128)(2,1)S(1)}, u32[]{:S(2)}, u32[]{:S(2)}) collective-permute-start(bf16[512,512]{1,0:T(8,128)(2,1)S(1)} %get-tuple-element.70), channel_id=1, source_target_pairs={{1,2},{3,4},{5,6},{7,8},{9,10},{11,12},{13,14},{15,16},{17,18},{19... | collective-permute-start | bytes 1572872 | tf_op jit(solution)/shard_map/ppermute | solution.py:318
  120.9 5.0 %collective-permute-start.9 = (bf16[512,512]{1,0:T(8,128)(2,1)S(1)}, bf16[512,512]{1,0:T(8,128)(2,1)S(1)}, u32[]{:S(2)}, u32[]{:S(2)}) collective-permute-start(bf16[512,512]{1,0:T(8,128)(2,1)S(1)} %shard_map.122), channel_id=1, source_target_pairs={{0,1},{2,3},{4,5},{6,7},{8,9},{10,11},{12,13},{14,15},{16,17},{18,... | collective-permute-start | bytes 1572872 | tf_op jit(solution)/shard_map/ppermute | solution.py:318
where the time goes:
time: 144 us
  Pallas kernels  63.8 us (44%)
  blocking collectives  53.1 us (37%)
  starting transfers between devices  14.3 us (10%)
  waiting for transfers between devices  10.6 us (7%)
    pallas_call x22, Pallas kernels, call(): pl.pallas_call(kernel, out_shape=[jax.ShapeDtypeStruct(*o) for o in outs]...  63.8 us
    all_to_all x4, blocking collectives, per_device(): got = lax.all_to_all(spread, 'sec', 0, 0)  53.1 us
    ppermute x8, starting transfers between devices, swapped(): return lax.ppermute(block, 'sec', pairs)  13.4 us
    ppermute x2, waiting for transfers between devices, per_device(): nb, inv = lax.ppermute((right_block[0, 0], inv_sv[0]), 'seg', route)  9.57 us
  transfers between devices with their start and end apart: 10, of which 3 were waited for; matrix products, arithmetic and copies ran while one was open for 0% of the time, Pallas kernels for 22%

commit v1 on v0

--- a/solution.py
+++ b/solution.py
@@ -11,6 +11,7 @@
 EPS = 1e-06
 ROWS = 64
 ROW = 1
+GROUP = 4
 MIB = 1 << 20
 BF16 = jnp.bfloat16
 F32 = jnp.float32
@@ -52,6 +53,34 @@
     @pl.when(lax.rem(count, 2) == 1)
     def _():
         acc[...] += term(lefts(last - 1, 0), 0)
+
+
+def apply_head(plan, x_ref, t_ref, sums, l_ref, r_ref, arrived=None):
+    n_far, head, _ = bounds(plan)
+    sums[...] = jnp.zeros_like(sums)
+
+    def group(start, size):
+        ws = []
+        for u in range(size):
+            w = plan[start + u] if arrived is None else arrived(start + u)
+            t_ref[u] = jnp.dot(l_ref[w], x_ref[...], preferred_element_type=F32).astype(BF16)
+            ws.append(w)
+        for u, w in enumerate(ws):
+            side = (start + u >= n_far).astype(jnp.int32)
+            sums[side] += lax.dot_general(
+                t_ref[u], r_ref[w], (((1,), (1,)), ((), ())), preferred_element_type=F32
+            )
+
+    def full(h, carry):
+        group(GROUP * h, GROUP)
+        return carry
+
+    lax.fori_loop(0, lax.div(head, GROUP), full, 0)
+    size = GROUP // 2
+    while size:
+        done = lax.div(head, 2 * size) * (2 * size)
+        pl.when(lax.rem(lax.div(head, size), 2) == 1)(functools.partial(group, done, size))
+        size //= 2
 
 
 def prepare_kernel(charge, far, dims, lb, precond, lb_out, inverse, plan, sems):
@@ -113,11 +142,11 @@
 
 
 def first_kernel(
-    plan, lb, nb, inv, l_hbm, r_hbm, x_ref, far_ref, near_part, uu_ref,
-    t_ref, acc, l_buf, r_buf, sems,
+    plan, lb, nb, inv, l_hbm, r_hbm, x_ref, far_ref, head_sums, uu_ref,
+    t_ref, l_buf, r_buf, sems,
 ):
     refs = (l_hbm, r_hbm, l_buf, r_buf, sems)
-    n_far, head, _ = bounds(plan)
+    head = bounds(plan)[1]
 
     def start(i, carry):
         for copy in env_copies(i, plan[i], refs):
@@ -136,11 +165,8 @@
             copy.wait()
         return i
 
-    acc[...] = jnp.zeros_like(acc)
-    near_part[...] = jnp.zeros_like(near_part)
-    apply_channels(plan, 0, n_far, x_ref, t_ref, acc, l_buf, r_buf, arrived)
-    far_ref[...] = acc[...].astype(BF16)
-    apply_channels(plan, n_far, head, x_ref, t_ref, near_part, l_buf, r_buf, arrived)
+    apply_head(plan, x_ref, t_ref, head_sums, l_buf, r_buf, arrived)
+    far_ref[...] = head_sums[0].astype(BF16)
 
 
 def at(red, lane):
@@ -193,16 +219,12 @@
     plan, got = refs[:2]
     older = refs[2 : 1 + k]
     basis = refs[1 + k : 1 + 2 * k]
-    image, inverse, l_ref, r_ref, x_ref, far_ref, near_part, red_ref, t_ref, acc = refs[1 + 2 * k :]
-    n_far, head, _ = bounds(plan)
+    image, inverse, l_ref, r_ref, x_ref, far_ref, head_sums, red_ref, t_ref = refs[1 + 2 * k :]
     red_ref[...] = summed(got, scale)
     reds = [r[...] for r in older] + [red_ref[...]]
     following(reds, image, inverse, basis, x_ref)
-    acc[...] = jnp.zeros_like(acc)
-    near_part[...] = jnp.zeros_like(near_part)
-    apply_channels(plan, 0, n_far, x_ref, t_ref, acc, l_ref, r_ref)
-    far_ref[...] = acc[...].astype(BF16)
-    apply_channels(plan, n_far, head, x_ref, t_ref, near_part, l_ref, r_ref)
+    apply_head(plan, x_ref, t_ref, head_sums, l_ref, r_ref)
+    far_ref[...] = head_sums[0].astype(BF16)
 
 
 def summed(got, scale):
@@ -233,9 +255,9 @@
     out.wait()
 
 
-def near_kernel(plan, x, near_part, l_ref, r_ref, near_ref, t_ref, acc):
+def near_kernel(plan, x, head_sums, l_ref, r_ref, near_ref, t_ref, acc):
     _, head, split = bounds(plan)
-    acc[...] = near_part[...]
+    acc[...] = head_sums[1]
     apply_channels(plan, head, split, x, t_ref, acc, l_ref, r_ref)
     near_ref[...] = acc[...].astype(BF16)
 
@@ -349,29 +371,30 @@
         [pltpu.SemaphoreType.DMA((2,))], MIB, 8,
     )
     scratch = [pltpu.VMEM((2, width, width), BF16), pltpu.VMEM(square, F32)]
+    head_scratch = [pltpu.VMEM((GROUP, width, width), BF16)]
     buffers = [pltpu.VMEM(lenv.shape, BF16)] * 2 + [pltpu.SemaphoreType.DMA((channels, 2))]
     basis, reds = [], []
     for k in range(MATVECS):
-        outs = [(square, BF16), (square, BF16), (square, F32), small]
+        outs = [(square, BF16), (square, BF16), ((2, width, width), F32), small]
         if k == 0:
-            x, to_far, near_part, guess_dots = call(
+            x, to_far, head_sums, guess_dots = call(
                 first_kernel,
                 (plan, left, nb, inv, *in_hbm(lenv, renv)),
                 [SMEM] + [VMEM] * 3 + [HBM] * 2,
-                outs, [VMEM] * 4, scratch + buffers, 20 * one, 24,
+                outs, [VMEM] * 4, head_scratch + buffers, 20 * one, 24,
             )
         else:
-            x, to_far, near_part, red = call(
+            x, to_far, head_sums, red = call(
                 functools.partial(next_kernel, k, scale),
                 (plan, got, *reds, *basis, image, inverse, lenv, renv),
                 [SMEM] + [VMEM] * (2 * k + 4),
-                outs, [VMEM] * 4, scratch, one, 16,
+                outs, [VMEM] * 4, head_scratch, one, 16,
             )
             reds.append(red)
         basis.append(x)
         from_far = swapped(to_far, far_pairs)
         (to_near,) = call(
-            near_kernel, (plan, x, near_part, lenv, renv), [SMEM] + [VMEM] * 4,
+            near_kernel, (plan, x, head_sums, lenv, renv), [SMEM] + [VMEM] * 4,
             [(square, BF16)], [VMEM], scratch, one, 16,
         )
         from_near = swapped(to_near, near_pairs)

time: 144 us -> 145 us (level); the launches traced: 144 us -> 143 us
  transfers between devices with their start and end apart: 10 -> 10, of which waited for: 3 -> 4; matrix products, arithmetic and copies ran while one was open for 0% -> 0% of each run, Pallas kernels for 22% -> 22%
where the time goes in v1:
time: 145 us; the launch traced here: 143 us
  Pallas kernels  62.9 us (43%)
  blocking collectives  52.5 us (36%)
  starting transfers between devices  14.1 us (10%)
  waiting for transfers between devices  11.3 us (8%)
    pallas_call x22, Pallas kernels, call(): pl.pallas_call(kernel, out_shape=[jax.ShapeDtypeStruct(*o) for o in outs]...  62.9 us
    all_to_all x4, blocking collectives, per_device(): got = lax.all_to_all(spread, 'sec', 0, 0)  52.5 us
    ppermute x8, starting transfers between devices, swapped(): return lax.ppermute(block, 'sec', pairs)  13.2 us
    ppermute x2, waiting for transfers between devices, per_device(): nb, inv = lax.ppermute((right_block[0, 0], inv_sv[0]), 'seg', route)  9.57 us
  transfers between devices with their start and end apart: 10, of which 4 were waited for; matrix products, arithmetic and copies ran while one was open for 0% of the time, Pallas kernels for 22%

profile of v1, /device:TPU:7, one launch (start us, length us, event | category | flops | bytes accessed | tf_op | source)
XLA Modules:
  0.0 143.2 jit_solution(14288065993796176779)
XLA Ops:
  0.6 0.6 collective-permute-start
  1.5 0.7 copy-done
  2.2 0.7 copy-done.1
  2.8 2.5 %shard_map.103 = (bf16[512,512]{1,0:T(8,128)(2,1)S(1)}, f32[512,512]{1,0:T(8,128)S(1)}, s32[18]{0:T(128)S(1)}) custom-call(s32[13]{0:T(128)S(1)} %copy-done, s32[1]{0:T(128)} %bitcast.far, s32[2]{0:T(128)S(1)} %bitcast.39, bf16[512,512]{1,0:T(8,128)(2,1)} %bitcast.41, f32[512,512]{1,0:T(8,128)} %bitcast.40), custom_call_target="tpu_custom_call" | custom-call | flops 1048576 | bytes 4196352 | tf_op jit(solution)/shard_map/pallas_call | solution.py:322
  5.4 9.6 %collective-permute-done.1.inv = bf16[1,512]{1,0:T(2,128)(2,1)S(1)} collective-permute-done((bf16[1,512]{1,0:T(2,128)(2,1)}, bf16[1,512]{1,0:T(2,128)(2,1)S(1)}, u32[]{:S(2)}, u32[]{:S(2)}) %collective-permute-start.1) | collective-permute-done | bytes 1056 | tf_op jit(solution)/shard_map/ppermute | solution.py:360
  15.0 5.9 %shard_map.104 = (bf16[512,512]{1,0:T(8,128)(2,1)S(1)}, bf16[512,512]{1,0:T(8,128)(2,1)S(1)}, f32[2,512,512]{2,1,0:T(8,128)S(1)}, f32[8,128]{1,0:T(8,128)S(1)}) custom-call(s32[18]{0:T(128)S(1)} %get-tuple-element.41.plan.refs_0_, bf16[512,512]{1,0:T(8,128)(2,1)S(1)} %get-tuple-element.42.lb, bf16[512,512]{1,0:T(8,128)(2,1)S(1)} %collective-permute-done.nb, ...), custom_call_target="tpu_custom_call" | custom-call | flops 46528811008 | bytes 95070888 | tf_op jit(solution)/shard_map/pallas_call | solution.py:322
  20.9 4.7 %collective-permute-start.2 = (bf16[512,512]{1,0:T(8,128)(2,1)S(1)}, bf16[512,512]{1,0:T(8,128)(2,1)S(1)}, u32[]{:S(2)}, u32[]{:S(2)}) collective-permute-start(bf16[512,512]{1,0:T(8,128)(2,1)S(1)} %get-tuple-element.46), channel_id=1, source_target_pairs={{1,2},{3,4},{5,6},{7,8},{9,10},{11,12},{13,14},{15,16},{17,18},{19... | collective-permute-start | bytes 1572872 | tf_op jit(solution)/shard_map/ppermute | solution.py:340
  25.6 1.9 %shard_map.107 = bf16[512,512]{1,0:T(8,128)(2,1)S(1)} custom-call(s32[18]{0:T(128)S(1)} %get-tuple-element.41.plan.refs_0_, bf16[512,512]{1,0:T(8,128)(2,1)S(1)} %get-tuple-element.43.refs_0_.x.refs_2_.refs_3_.refs_4_, f32[2,512,512]{2,1,0:T(8,128)S(1)} %get-tuple-element.47.head_sums, bf16[13,512,512]{2,1,0:T(8,128)(2,1)S(1)} %bitcast.14, ...), custom_call_target="tpu_custom_call" | custom-call | flops 2326440704 | bytes 8738133 | tf_op jit(solution)/shard_map/pallas_call | solution.py:322
  27.6 4.8 %shard_map.105 = (f32[512,512]{1,0:T(8,128)S(1)}, f32[8,128]{1,0:T(8,128)S(1)}) custom-call(s32[18]{0:T(128)S(1)} %get-tuple-element.41.plan.refs_0_, bf16[512,512]{1,0:T(8,128)(2,1)S(1)} %get-tuple-element.43.refs_0_.x.refs_2_.refs_3_.refs_4_, f32[512,512]{1,0:T(8,128)S(1)} %get-tuple-element.44.refs_1_.refs_3_.refs_4_.refs_2_.refs_6_.refs_5_.refs_8_.refs_9_, ...), custom_call_target="tpu_custom_call" | custom-call | flops 2326440704 | bytes 8738133 | tf_op jit(solution)/shard_map/pallas_call | solution.py:322
  32.5 1.3 shard_map.108
  33.9 15.7 %all_to_all.20.refs_1_ = f32[32,1,128]{2,1,0:T(1,128)S(1)} all-to-all(f32[32,1,128]{2,1,0:T(1,128)S(1)} %get-tuple-element.50), channel_id=1, replica_groups=mesh['seg'=4,'sec'=32] {'sec'}, dimensions={0} | all-to-all | bytes 32768 | tf_op jit(solution)/shard_map/all_to_all | solution.py:419
  49.6 5.3 %shard_map.109 = (bf16[512,512]{1,0:T(8,128)(2,1)S(1)}, bf16[512,512]{1,0:T(8,128)(2,1)S(1)}, f32[2,512,512]{2,1,0:T(8,128)S(1)}, f32[8,128]{1,0:T(8,128)S(1)}) custom-call(s32[18]{0:T(128)S(1)} %get-tuple-element.41.plan.refs_0_, f32[32,1,128]{2,1,0:T(1,128)S(1)} %all_to_all.20.refs_1_, ...), custom_call_target="tpu_custom_call" | custom-call | flops 2326440704 | bytes 8738133 | tf_op jit(solution)/shard_map/pallas_call | solution.py:322
  54.8 2.7 %collective-permute-start.4 = (bf16[512,512]{1,0:T(8,128)(2,1)S(1)}, bf16[512,512]{1,0:T(8,128)(2,1)S(1)}, u32[]{:S(2)}, u32[]{:S(2)}) collective-permute-start(bf16[512,512]{1,0:T(8,128)(2,1)S(1)} %get-tuple-element.54), channel_id=1, source_target_pairs={{1,2},{3,4},{5,6},{7,8},{9,10},{11,12},{13,14},{15,16},{17,18},{19... | collective-permute-start | bytes 1572872 | tf_op jit(solution)/shard_map/ppermute | solution.py:340
  57.6 2.1 %shard_map.112 = bf16[512,512]{1,0:T(8,128)(2,1)S(1)} custom-call(s32[18]{0:T(128)S(1)} %get-tuple-element.41.plan.refs_0_, bf16[512,512]{1,0:T(8,128)(2,1)S(1)} %get-tuple-element.52.refs_1_.x.refs_4_.refs_5_, f32[2,512,512]{2,1,0:T(8,128)S(1)} %get-tuple-element.55.head_sums, bf16[13,512,512]{2,1,0:T(8,128)(2,1)S(1)} %bitcast.17, ...), custom_call_target="tpu_custom_call" | custom-call | flops 2326440704 | bytes 8738133 | tf_op jit(solution)/shard_map/pallas_call | solution.py:322
  59.8 4.9 %shard_map.110 = (f32[512,512]{1,0:T(8,128)S(1)}, f32[8,128]{1,0:T(8,128)S(1)}) custom-call(s32[18]{0:T(128)S(1)} %get-tuple-element.41.plan.refs_0_, bf16[512,512]{1,0:T(8,128)(2,1)S(1)} %get-tuple-element.43.refs_0_.x.refs_2_.refs_3_.refs_4_, bf16[512,512]{1,0:T(8,128)(2,1)S(1)} %get-tuple-element.52.refs_1_.x.refs_4_.refs_5_, ...), custom_call_target="tpu_custom_call" | custom-call | flops 2326440704 | bytes 8738133 | tf_op jit(solution)/shard_map/pallas_call | solution.py:322
  64.7 0.6 collective-permute-done.4.from_far
  65.4 1.5 %shard_map.113 = (f32[512,512]{1,0:T(8,128)S(1)}, f32[32,1,128]{2,1,0:T(1,128)S(1)}) custom-call(s32[18]{0:T(128)S(1)} %get-tuple-element.41.plan.refs_0_, bf16[512,512]{1,0:T(8,128)(2,1)S(1)} %get-tuple-element.43.refs_0_.x.refs_2_.refs_3_.refs_4_, bf16[512,512]{1,0:T(8,128)(2,1)S(1)} %get-tuple-element.52.refs_1_.x.refs_4_.refs_5_, ...), custom_call_target="tpu_custom_call" | custom-call | flops 1048576 | bytes 4196352 | tf_op jit(solution)/shard_map/pallas_call | solution.py:322
  66.9 12.2 %all_to_all.21.refs_1_ = f32[32,1,128]{2,1,0:T(1,128)S(1)} all-to-all(f32[32,1,128]{2,1,0:T(1,128)S(1)} %get-tuple-element.57), channel_id=1, replica_groups=mesh['seg'=4,'sec'=32] {'sec'}, dimensions={0} | all-to-all | bytes 32768 | tf_op jit(solution)/shard_map/all_to_all | solution.py:419
  79.1 5.4 %shard_map.114 = (bf16[512,512]{1,0:T(8,128)(2,1)S(1)}, bf16[512,512]{1,0:T(8,128)(2,1)S(1)}, f32[2,512,512]{2,1,0:T(8,128)S(1)}, f32[8,128]{1,0:T(8,128)S(1)}) custom-call(s32[18]{0:T(128)S(1)} %get-tuple-element.41.plan.refs_0_, f32[32,1,128]{2,1,0:T(1,128)S(1)} %all_to_all.21.refs_1_, f32[8,128]{1,0:T(8,128)S(1)} %get-tuple-element.58.refs_2_.refs_1_, ...), custom_call_target="tpu_custom_call" | custom-call | flops 2326440704 | bytes 8738133 | tf_op jit(solution)/shard_map/pallas_call | solution.py:322
  84.5 2.7 %collective-permute-start.6 = (bf16[512,512]{1,0:T(8,128)(2,1)S(1)}, bf16[512,512]{1,0:T(8,128)(2,1)S(1)}, u32[]{:S(2)}, u32[]{:S(2)}) collective-permute-start(bf16[512,512]{1,0:T(8,128)(2,1)S(1)} %get-tuple-element.62), channel_id=1, source_target_pairs={{1,2},{3,4},{5,6},{7,8},{9,10},{11,12},{13,14},{15,16},{17,18},{19... | collective-permute-start | bytes 1572872 | tf_op jit(solution)/shard_map/ppermute | solution.py:340
  87.2 1.9 %shard_map.117 = bf16[512,512]{1,0:T(8,128)(2,1)S(1)} custom-call(s32[18]{0:T(128)S(1)} %get-tuple-element.41.plan.refs_0_, bf16[512,512]{1,0:T(8,128)(2,1)S(1)} %get-tuple-element.60.refs_2_.x.refs_6_, f32[2,512,512]{2,1,0:T(8,128)S(1)} %get-tuple-element.63.head_sums, bf16[13,512,512]{2,1,0:T(8,128)(2,1)S(1)} %bitcast.20, bf16[13,512,512]{2,1,0:T(8,128)(2,1)S(1)} %bitcast.34), custom_call_target="tpu_custom_call" | custom-call | flops 2326440704 | bytes 8738133 | tf_op jit(solution)/shard_map/pallas_call | solution.py:322
  89.3 5.1 %shard_map.115 = (f32[512,512]{1,0:T(8,128)S(1)}, f32[8,128]{1,0:T(8,128)S(1)}) custom-call(s32[18]{0:T(128)S(1)} %get-tuple-element.41.plan.refs_0_, bf16[512,512]{1,0:T(8,128)(2,1)S(1)} %get-tuple-element.43.refs_0_.x.refs_2_.refs_3_.refs_4_, bf16[512,512]{1,0:T(8,128)(2,1)S(1)} %get-tuple-element.52.refs_1_.x.refs_4_.refs_5_, ...), custom_call_target="tpu_custom_call" | custom-call | flops 2326440704 | bytes 8738133 | tf_op jit(solution)/shard_map/pallas_call | solution.py:322
  94.4 0.6 collective-permute-done.6.from_far
  95.1 1.7 %shard_map.118 = (f32[512,512]{1,0:T(8,128)S(1)}, f32[32,1,128]{2,1,0:T(1,128)S(1)}) custom-call(s32[18]{0:T(128)S(1)} %get-tuple-element.41.plan.refs_0_, bf16[512,512]{1,0:T(8,128)(2,1)S(1)} %get-tuple-element.43.refs_0_.x.refs_2_.refs_3_.refs_4_, bf16[512,512]{1,0:T(8,128)(2,1)S(1)} %get-tuple-element.52.refs_1_.x.refs_4_.refs_5_, ...), custom_call_target="tpu_custom_call" | custom-call | flops 1048576 | bytes 4196352 | tf_op jit(solution)/shard_map/pallas_call | solution.py:322
  96.8 12.2 %all_to_all.22.refs_1_ = f32[32,1,128]{2,1,0:T(1,128)S(1)} all-to-all(f32[32,1,128]{2,1,0:T(1,128)S(1)} %get-tuple-element.65), channel_id=1, replica_groups=mesh['seg'=4,'sec'=32] {'sec'}, dimensions={0} | all-to-all | bytes 32768 | tf_op jit(solution)/shard_map/all_to_all | solution.py:419
  109.0 5.8 %shard_map.119 = (bf16[512,512]{1,0:T(8,128)(2,1)S(1)}, bf16[512,512]{1,0:T(8,128)(2,1)S(1)}, f32[2,512,512]{2,1,0:T(8,128)S(1)}, f32[8,128]{1,0:T(8,128)S(1)}) custom-call(s32[18]{0:T(128)S(1)} %get-tuple-element.41.plan.refs_0_, f32[32,1,128]{2,1,0:T(1,128)S(1)} %all_to_all.22.refs_1_, f32[8,128]{1,0:T(8,128)S(1)} %get-tuple-element.58.refs_2_.refs_1_, ...), custom_call_target="tpu_custom_call" | custom-call | flops 2326440704 | bytes 8738133 | tf_op jit(solution)/shard_map/pallas_call | solution.py:322
  114.8 2.7 %collective-permute-start.8 = (bf16[512,512]{1,0:T(8,128)(2,1)S(1)}, bf16[512,512]{1,0:T(8,128)(2,1)S(1)}, u32[]{:S(2)}, u32[]{:S(2)}) collective-permute-start(bf16[512,512]{1,0:T(8,128)(2,1)S(1)} %get-tuple-element.70), channel_id=1, source_target_pairs={{1,2},{3,4},{5,6},{7,8},{9,10},{11,12},{13,14},{15,16},{17,18},{19... | collective-permute-start | bytes 1572872 | tf_op jit(solution)/shard_map/ppermute | solution.py:340
  117.6 1.9 %shard_map.122 = bf16[512,512]{1,0:T(8,128)(2,1)S(1)} custom-call(s32[18]{0:T(128)S(1)} %get-tuple-element.41.plan.refs_0_, bf16[512,512]{1,0:T(8,128)(2,1)S(1)} %get-tuple-element.68.refs_3_.x.refs_7_, f32[2,512,512]{2,1,0:T(8,128)S(1)} %get-tuple-element.71.head_sums, bf16[13,512,512]{2,1,0:T(8,128)(2,1)S(1)} %bitcast.23, bf16[13,512,512]{2,1,0:T(8,128)(2,1)S(1)} %bitcast.37), custom_call_target="tpu_custom_call" | custom-call | flops 2326440704 | bytes 8738133 | tf_op jit(solution)/shard_map/pallas_call | solution.py:322
  119.6 5.3 %shard_map.120 = (f32[512,512]{1,0:T(8,128)S(1)}, f32[8,128]{1,0:T(8,128)S(1)}) custom-call(s32[18]{0:T(128)S(1)} %get-tuple-element.41.plan.refs_0_, bf16[512,512]{1,0:T(8,128)(2,1)S(1)} %get-tuple-element.43.refs_0_.x.refs_2_.refs_3_.refs_4_, bf16[512,512]{1,0:T(8,128)(2,1)S(1)} %get-tuple-element.52.refs_1_.x.refs_4_.refs_5_, ...), custom_call_target="tpu_custom_call" | custom-call | flops 2326440704 | bytes 8738133 | tf_op jit(solution)/shard_map/pallas_call | solution.py:322
  125.4 2.0 %shard_map.123 = (f32[512,512]{1,0:T(8,128)S(1)}, f32[32,1,128]{2,1,0:T(1,128)S(1)}) custom-call(s32[18]{0:T(128)S(1)} %get-tuple-element.41.plan.refs_0_, bf16[512,512]{1,0:T(8,128)(2,1)S(1)} %get-tuple-element.43.refs_0_.x.refs_2_.refs_3_.refs_4_, bf16[512,512]{1,0:T(8,128)(2,1)S(1)} %get-tuple-element.52.refs_1_.x.refs_4_.refs_5_, ...), custom_call_target="tpu_custom_call" | custom-call | flops 1048576 | bytes 4196352 | tf_op jit(solution)/shard_map/pallas_call | solution.py:322
  127.4 12.4 %all_to_all.23.refs_0_ = f32[32,1,128]{2,1,0:T(1,128)S(1)} all-to-all(f32[32,1,128]{2,1,0:T(1,128)S(1)} %get-tuple-element.73), channel_id=1, replica_groups=mesh['seg'=4,'sec'=32] {'sec'}, dimensions={0} | all-to-all | bytes 32768 | tf_op jit(solution)/shard_map/all_to_all | solution.py:419
  139.8 3.2 %shard_map.124 = (bf16[512,512]{1,0:T(8,128)(2,1)}, f32[512,512]{1,0:T(8,128)}, f32[4,4]{1,0:T(4,128)}) custom-call(f32[32,1,128]{2,1,0:T(1,128)S(1)} %all_to_all.23.refs_0_, f32[8,128]{1,0:T(8,128)S(1)} %get-tuple-element.58.refs_2_.refs_1_, f32[8,128]{1,0:T(8,128)S(1)} %get-tuple-element.66.refs_3_.refs_2_, f32[8,128]{1,0:T(8,128)S(1)} %get-tuple-element.74.refs_3_, ...), custom_call_target="tpu_custom_call" | custom-call | flops 1048576 | bytes 4196352 | tf_op jit(solution)/shard_map/pallas_call | solution.py:322
  (28 shorter events, 1.5 us)
Async XLA Ops:
  0.6 14.3 %collective-permute-start = (bf16[512,512]{1,0:T(8,128)(2,1)}, bf16[512,512]{1,0:T(8,128)(2,1)S(1)}, u32[]{:S(2)}, u32[]{:S(2)}) collective-permute-start(bf16[512,512]{1,0:T(8,128)(2,1)} %bitcast.43), channel_id=1, source_target_pairs={{32,0},{64,32},{96,64},{0,96},{33,1},{65,33},{97,65},{1,97},{34,2}... | collective-permute-start | bytes 1572872 | tf_op jit(solution)/shard_map/ppermute | solution.py:360
  1.2 13.7 %collective-permute-start.1 = (bf16[1,512]{1,0:T(2,128)(2,1)}, bf16[1,512]{1,0:T(2,128)(2,1)S(1)}, u32[]{:S(2)}, u32[]{:S(2)}) collective-permute-start(bf16[1,512]{1,0:T(2,128)(2,1)} %bitcast.45), channel_id=1, source_target_pairs={{32,0},{64,32},{96,64},{0,96},{33,1},{65,33},{97,65},{1,97},{34,2}... | collective-permute-start | bytes 3080 | tf_op jit(solution)/shard_map/ppermute | solution.py:360
  1.5 0.7 copy-start
  2.2 0.7 copy-start.1
  14.9 10.6 %slice-start = ((s8[6815744]{0:T(1024)(128)(4,1)}), s8[4194304]{0:T(1024)(128)(4,1)S(1)}, s32[]{:S(2)}) async-start(s8[6815744]{0:T(1024)(128)(4,1)} %bitcast.12), calls=%async_computation.4 | async-start | bytes 8388608
  14.9 10.6 %slice-start.2 = ((s8[6815744]{0:T(1024)(128)(4,1)}), s8[4194304]{0:T(1024)(128)(4,1)S(1)}, s32[]{:S(2)}) async-start(s8[6815744]{0:T(1024)(128)(4,1)} %bitcast.26), calls=%async_computation.6 | async-start | bytes 8388608
  14.9 10.6 %slice-start.1 = ((s8[6815744]{0:T(1024)(128)(4,1)}), s8[2621440]{0:T(1024)(128)(4,1)S(1)}, s32[]{:S(2)}) async-start(s8[6815744]{0:T(1024)(128)(4,1)} %bitcast.12), calls=%async_computation.5 | async-start | bytes 5242880
  14.9 10.6 %slice-start.3 = ((s8[6815744]{0:T(1024)(128)(4,1)}), s8[2621440]{0:T(1024)(128)(4,1)S(1)}, s32[]{:S(2)}) async-start(s8[6815744]{0:T(1024)(128)(4,1)} %bitcast.26), calls=%async_computation.7 | async-start | bytes 5242880
  20.9 11.5 %collective-permute-start.2 = (bf16[512,512]{1,0:T(8,128)(2,1)S(1)}, bf16[512,512]{1,0:T(8,128)(2,1)S(1)}, u32[]{:S(2)}, u32[]{:S(2)}) collective-permute-start(bf16[512,512]{1,0:T(8,128)(2,1)S(1)} %get-tuple-element.46), channel_id=1, source_target_pairs={{1,2},{3,4},{5,6},{7,8},{9,10},{11,12},{13,14},{15,16},{17,18},{19... | collective-permute-start | bytes 1572872 | tf_op jit(solution)/shard_map/ppermute | solution.py:340
  27.5 5.0 %collective-permute-start.3 = (bf16[512,512]{1,0:T(8,128)(2,1)S(1)}, bf16[512,512]{1,0:T(8,128)(2,1)S(1)}, u32[]{:S(2)}, u32[]{:S(2)}) collective-permute-start(bf16[512,512]{1,0:T(8,128)(2,1)S(1)} %shard_map.107), channel_id=1, source_target_pairs={{0,1},{2,3},{4,5},{6,7},{8,9},{10,11},{12,13},{14,15},{16,17},{18,... | collective-permute-start | bytes 1572872 | tf_op jit(solution)/shard_map/ppermute | solution.py:340
  54.8 10.5 %collective-permute-start.4 = (bf16[512,512]{1,0:T(8,128)(2,1)S(1)}, bf16[512,512]{1,0:T(8,128)(2,1)S(1)}, u32[]{:S(2)}, u32[]{:S(2)}) collective-permute-start(bf16[512,512]{1,0:T(8,128)(2,1)S(1)} %get-tuple-element.54), channel_id=1, source_target_pairs={{1,2},{3,4},{5,6},{7,8},{9,10},{11,12},{13,14},{15,16},{17,18},{19... | collective-permute-start | bytes 1572872 | tf_op jit(solution)/shard_map/ppermute | solution.py:340
  59.7 5.7 %collective-permute-start.5 = (bf16[512,512]{1,0:T(8,128)(2,1)S(1)}, bf16[512,512]{1,0:T(8,128)(2,1)S(1)}, u32[]{:S(2)}, u32[]{:S(2)}) collective-permute-start(bf16[512,512]{1,0:T(8,128)(2,1)S(1)} %shard_map.112), channel_id=1, source_target_pairs={{0,1},{2,3},{4,5},{6,7},{8,9},{10,11},{12,13},{14,15},{16,17},{18,... | collective-permute-start | bytes 1572872 | tf_op jit(solution)/shard_map/ppermute | solution.py:340
  84.5 10.5 %collective-permute-start.6 = (bf16[512,512]{1,0:T(8,128)(2,1)S(1)}, bf16[512,512]{1,0:T(8,128)(2,1)S(1)}, u32[]{:S(2)}, u32[]{:S(2)}) collective-permute-start(bf16[512,512]{1,0:T(8,128)(2,1)S(1)} %get-tuple-element.62), channel_id=1, source_target_pairs={{1,2},{3,4},{5,6},{7,8},{9,10},{11,12},{13,14},{15,16},{17,18},{19... | collective-permute-start | bytes 1572872 | tf_op jit(solution)/shard_map/ppermute | solution.py:340
  89.2 6.0 %collective-permute-start.7 = (bf16[512,512]{1,0:T(8,128)(2,1)S(1)}, bf16[512,512]{1,0:T(8,128)(2,1)S(1)}, u32[]{:S(2)}, u32[]{:S(2)}) collective-permute-start(bf16[512,512]{1,0:T(8,128)(2,1)S(1)} %shard_map.117), channel_id=1, source_target_pairs={{0,1},{2,3},{4,5},{6,7},{8,9},{10,11},{12,13},{14,15},{16,17},{18,... | collective-permute-start | bytes 1572872 | tf_op jit(solution)/shard_map/ppermute | solution.py:340
  114.8 10.5 %collective-permute-start.8 = (bf16[512,512]{1,0:T(8,128)(2,1)S(1)}, bf16[512,512]{1,0:T(8,128)(2,1)S(1)}, u32[]{:S(2)}, u32[]{:S(2)}) collective-permute-start(bf16[512,512]{1,0:T(8,128)(2,1)S(1)} %get-tuple-element.70), channel_id=1, source_target_pairs={{1,2},{3,4},{5,6},{7,8},{9,10},{11,12},{13,14},{15,16},{17,18},{19... | collective-permute-start | bytes 1572872 | tf_op jit(solution)/shard_map/ppermute | solution.py:340
  119.5 5.9 %collective-permute-start.9 = (bf16[512,512]{1,0:T(8,128)(2,1)S(1)}, bf16[512,512]{1,0:T(8,128)(2,1)S(1)}, u32[]{:S(2)}, u32[]{:S(2)}) collective-permute-start(bf16[512,512]{1,0:T(8,128)(2,1)S(1)} %shard_map.122), channel_id=1, source_target_pairs={{0,1},{2,3},{4,5},{6,7},{8,9},{10,11},{12,13},{14,15},{16,17},{18,... | collective-permute-start | bytes 1572872 | tf_op jit(solution)/shard_map/ppermute | solution.py:340

commit v2 on v1

--- a/solution.py
+++ b/solution.py
@@ -9,7 +9,7 @@
 
 MATVECS = 4
 EPS = 1e-06
-ROWS = 64
+ROWS = 32
 ROW = 1
 GROUP = 4
 MIB = 1 << 20

time: 145 us -> 148 us (1.021); the launches traced: 143 us -> 149 us
  Pallas kernels: 62.9 us -> 67.1 us
  waiting for transfers between devices: 11.3 us -> 13 us
    pallas_call x22, Pallas kernels: 62.9 us -> 67.1 us  [call(): pl.pallas_call(kernel, out_shape=[jax.ShapeDtypeStruct(*o) for o in outs]...]
    ppermute x8, waiting for transfers between devices: 1.71 us -> 3.45 us  [swapped(): return lax.ppermute(block, 'sec', pairs)]
  transfers between devices with their start and end apart: 10 -> 10, of which waited for: 4 -> 5; matrix products, arithmetic and copies ran while one was open for 0% -> 0% of each run, Pallas kernels for 22% -> 20%
where the time goes in v2:
time: 148 us; the launch traced here: 149 us
  Pallas kernels  67.1 us (45%)
  blocking collectives  52.2 us (35%)
  starting transfers between devices  14.1 us (10%)
  waiting for transfers between devices  13 us (9%)
    pallas_call x22, Pallas kernels, call(): pl.pallas_call(kernel, out_shape=[jax.ShapeDtypeStruct(*o) for o in outs]...  67.1 us
    all_to_all x4, blocking collectives, per_device(): got = lax.all_to_all(spread, 'sec', 0, 0)  52.2 us
    ppermute x8, starting transfers between devices, swapped(): return lax.ppermute(block, 'sec', pairs)  13.2 us
    ppermute x2, waiting for transfers between devices, per_device(): nb, inv = lax.ppermute((right_block[0, 0], inv_sv[0]), 'seg', route)  9.57 us
    ppermute x8, waiting for transfers between devices, swapped(): return lax.ppermute(block, 'sec', pairs)  3.45 us
  transfers between devices with their start and end apart: 10, of which 5 were waited for; matrix products, arithmetic and copies ran while one was open for 0% of the time, Pallas kernels for 20%

profile of v2, /device:TPU:7, one launch (start us, length us, event | category | flops | bytes accessed | tf_op | source)
XLA Modules:
  0.0 148.8 jit_solution(1804642650711080421)
XLA Ops:
  1.5 0.7 copy-done
  2.2 0.7 copy-done.1
  2.8 2.5 %shard_map.103 = (bf16[512,512]{1,0:T(8,128)(2,1)S(1)}, f32[512,512]{1,0:T(8,128)S(1)}, s32[18]{0:T(128)S(1)}) custom-call(s32[13]{0:T(128)S(1)} %copy-done, s32[1]{0:T(128)} %bitcast.far, s32[2]{0:T(128)S(1)} %bitcast.39, bf16[512,512]{1,0:T(8,128)(2,1)} %bitcast.41, f32[512,512]{1,0:T(8,128)} %bitcast.40), custom_call_target="tpu_custom_call" | custom-call | flops 1048576 | bytes 4196352 | tf_op jit(solution)/shard_map/pallas_call | solution.py:322
  5.4 9.6 %collective-permute-done.1.inv = bf16[1,512]{1,0:T(2,128)(2,1)S(1)} collective-permute-done((bf16[1,512]{1,0:T(2,128)(2,1)}, bf16[1,512]{1,0:T(2,128)(2,1)S(1)}, u32[]{:S(2)}, u32[]{:S(2)}) %collective-permute-start.1) | collective-permute-done | bytes 1056 | tf_op jit(solution)/shard_map/ppermute | solution.py:360
  15.0 6.6 %shard_map.104 = (bf16[512,512]{1,0:T(8,128)(2,1)S(1)}, bf16[512,512]{1,0:T(8,128)(2,1)S(1)}, f32[2,512,512]{2,1,0:T(8,128)S(1)}, f32[8,128]{1,0:T(8,128)S(1)}) custom-call(s32[18]{0:T(128)S(1)} %get-tuple-element.41.plan.refs_0_, bf16[512,512]{1,0:T(8,128)(2,1)S(1)} %get-tuple-element.42.lb, bf16[512,512]{1,0:T(8,128)(2,1)S(1)} %collective-permute-done.nb, ...), custom_call_target="tpu_custom_call" | custom-call | flops 46528811008 | bytes 95070888 | tf_op jit(solution)/shard_map/pallas_call | solution.py:322
  21.6 4.7 %collective-permute-start.2 = (bf16[512,512]{1,0:T(8,128)(2,1)S(1)}, bf16[512,512]{1,0:T(8,128)(2,1)S(1)}, u32[]{:S(2)}, u32[]{:S(2)}) collective-permute-start(bf16[512,512]{1,0:T(8,128)(2,1)S(1)} %get-tuple-element.46), channel_id=1, source_target_pairs={{1,2},{3,4},{5,6},{7,8},{9,10},{11,12},{13,14},{15,16},{17,18},{19... | collective-permute-start | bytes 1572872 | tf_op jit(solution)/shard_map/ppermute | solution.py:340
  26.3 3.2 %shard_map.107 = bf16[512,512]{1,0:T(8,128)(2,1)S(1)} custom-call(s32[18]{0:T(128)S(1)} %get-tuple-element.41.plan.refs_0_, bf16[512,512]{1,0:T(8,128)(2,1)S(1)} %get-tuple-element.43.refs_0_.x.refs_2_.refs_3_.refs_4_, f32[2,512,512]{2,1,0:T(8,128)S(1)} %get-tuple-element.47.head_sums, bf16[13,512,512]{2,1,0:T(8,128)(2,1)S(1)} %bitcast.14, ...), custom_call_target="tpu_custom_call" | custom-call | flops 2326440704 | bytes 8738133 | tf_op jit(solution)/shard_map/pallas_call | solution.py:322
  29.6 3.0 %shard_map.105 = (f32[512,512]{1,0:T(8,128)S(1)}, f32[8,128]{1,0:T(8,128)S(1)}) custom-call(s32[18]{0:T(128)S(1)} %get-tuple-element.41.plan.refs_0_, bf16[512,512]{1,0:T(8,128)(2,1)S(1)} %get-tuple-element.43.refs_0_.x.refs_2_.refs_3_.refs_4_, f32[512,512]{1,0:T(8,128)S(1)} %get-tuple-element.44.refs_1_.refs_3_.refs_4_.refs_2_.refs_6_.refs_5_.refs_8_.refs_9_, ...), custom_call_target="tpu_custom_call" | custom-call | flops 2326440704 | bytes 8738133 | tf_op jit(solution)/shard_map/pallas_call | solution.py:322
  33.2 1.4 shard_map.108
  34.6 15.7 %all_to_all.20.refs_1_ = f32[32,1,128]{2,1,0:T(1,128)S(1)} all-to-all(f32[32,1,128]{2,1,0:T(1,128)S(1)} %get-tuple-element.50), channel_id=1, replica_groups=mesh['seg'=4,'sec'=32] {'sec'}, dimensions={0} | all-to-all | bytes 32768 | tf_op jit(solution)/shard_map/all_to_all | solution.py:419
  50.3 6.6 %shard_map.109 = (bf16[512,512]{1,0:T(8,128)(2,1)S(1)}, bf16[512,512]{1,0:T(8,128)(2,1)S(1)}, f32[2,512,512]{2,1,0:T(8,128)S(1)}, f32[8,128]{1,0:T(8,128)S(1)}) custom-call(s32[18]{0:T(128)S(1)} %get-tuple-element.41.plan.refs_0_, f32[32,1,128]{2,1,0:T(1,128)S(1)} %all_to_all.20.refs_1_, ...), custom_call_target="tpu_custom_call" | custom-call | flops 2326440704 | bytes 8738133 | tf_op jit(solution)/shard_map/pallas_call | solution.py:322
  56.9 2.7 %collective-permute-start.4 = (bf16[512,512]{1,0:T(8,128)(2,1)S(1)}, bf16[512,512]{1,0:T(8,128)(2,1)S(1)}, u32[]{:S(2)}, u32[]{:S(2)}) collective-permute-start(bf16[512,512]{1,0:T(8,128)(2,1)S(1)} %get-tuple-element.54), channel_id=1, source_target_pairs={{1,2},{3,4},{5,6},{7,8},{9,10},{11,12},{13,14},{15,16},{17,18},{19... | collective-permute-start | bytes 1572872 | tf_op jit(solution)/shard_map/ppermute | solution.py:340
  59.6 3.4 %shard_map.112 = bf16[512,512]{1,0:T(8,128)(2,1)S(1)} custom-call(s32[18]{0:T(128)S(1)} %get-tuple-element.41.plan.refs_0_, bf16[512,512]{1,0:T(8,128)(2,1)S(1)} %get-tuple-element.52.refs_1_.x.refs_4_.refs_5_, f32[2,512,512]{2,1,0:T(8,128)S(1)} %get-tuple-element.55.head_sums, bf16[13,512,512]{2,1,0:T(8,128)(2,1)S(1)} %bitcast.17, ...), custom_call_target="tpu_custom_call" | custom-call | flops 2326440704 | bytes 8738133 | tf_op jit(solution)/shard_map/pallas_call | solution.py:322
  63.1 3.2 %shard_map.110 = (f32[512,512]{1,0:T(8,128)S(1)}, f32[8,128]{1,0:T(8,128)S(1)}) custom-call(s32[18]{0:T(128)S(1)} %get-tuple-element.41.plan.refs_0_, bf16[512,512]{1,0:T(8,128)(2,1)S(1)} %get-tuple-element.43.refs_0_.x.refs_2_.refs_3_.refs_4_, bf16[512,512]{1,0:T(8,128)(2,1)S(1)} %get-tuple-element.52.refs_1_.x.refs_4_.refs_5_, ...), custom_call_target="tpu_custom_call" | custom-call | flops 2326440704 | bytes 8738133 | tf_op jit(solution)/shard_map/pallas_call | solution.py:322
  66.3 1.1 collective-permute-done.4.from_far
  67.5 1.6 %shard_map.113 = (f32[512,512]{1,0:T(8,128)S(1)}, f32[32,1,128]{2,1,0:T(1,128)S(1)}) custom-call(s32[18]{0:T(128)S(1)} %get-tuple-element.41.plan.refs_0_, bf16[512,512]{1,0:T(8,128)(2,1)S(1)} %get-tuple-element.43.refs_0_.x.refs_2_.refs_3_.refs_4_, bf16[512,512]{1,0:T(8,128)(2,1)S(1)} %get-tuple-element.52.refs_1_.x.refs_4_.refs_5_, ...), custom_call_target="tpu_custom_call" | custom-call | flops 1048576 | bytes 4196352 | tf_op jit(solution)/shard_map/pallas_call | solution.py:322
  69.1 12.2 %all_to_all.21.refs_1_ = f32[32,1,128]{2,1,0:T(1,128)S(1)} all-to-all(f32[32,1,128]{2,1,0:T(1,128)S(1)} %get-tuple-element.57), channel_id=1, replica_groups=mesh['seg'=4,'sec'=32] {'sec'}, dimensions={0} | all-to-all | bytes 32768 | tf_op jit(solution)/shard_map/all_to_all | solution.py:419
  81.3 6.7 %shard_map.114 = (bf16[512,512]{1,0:T(8,128)(2,1)S(1)}, bf16[512,512]{1,0:T(8,128)(2,1)S(1)}, f32[2,512,512]{2,1,0:T(8,128)S(1)}, f32[8,128]{1,0:T(8,128)S(1)}) custom-call(s32[18]{0:T(128)S(1)} %get-tuple-element.41.plan.refs_0_, f32[32,1,128]{2,1,0:T(1,128)S(1)} %all_to_all.21.refs_1_, f32[8,128]{1,0:T(8,128)S(1)} %get-tuple-element.58.refs_2_.refs_1_, ...), custom_call_target="tpu_custom_call" | custom-call | flops 2326440704 | bytes 8738133 | tf_op jit(solution)/shard_map/pallas_call | solution.py:322
  88.0 2.7 %collective-permute-start.6 = (bf16[512,512]{1,0:T(8,128)(2,1)S(1)}, bf16[512,512]{1,0:T(8,128)(2,1)S(1)}, u32[]{:S(2)}, u32[]{:S(2)}) collective-permute-start(bf16[512,512]{1,0:T(8,128)(2,1)S(1)} %get-tuple-element.62), channel_id=1, source_target_pairs={{1,2},{3,4},{5,6},{7,8},{9,10},{11,12},{13,14},{15,16},{17,18},{19... | collective-permute-start | bytes 1572872 | tf_op jit(solution)/shard_map/ppermute | solution.py:340
  90.7 3.2 %shard_map.117 = bf16[512,512]{1,0:T(8,128)(2,1)S(1)} custom-call(s32[18]{0:T(128)S(1)} %get-tuple-element.41.plan.refs_0_, bf16[512,512]{1,0:T(8,128)(2,1)S(1)} %get-tuple-element.60.refs_2_.x.refs_6_, f32[2,512,512]{2,1,0:T(8,128)S(1)} %get-tuple-element.63.head_sums, bf16[13,512,512]{2,1,0:T(8,128)(2,1)S(1)} %bitcast.20, bf16[13,512,512]{2,1,0:T(8,128)(2,1)S(1)} %bitcast.34), custom_call_target="tpu_custom_call" | custom-call | flops 2326440704 | bytes 8738133 | tf_op jit(solution)/shard_map/pallas_call | solution.py:322
  94.0 3.4 %shard_map.115 = (f32[512,512]{1,0:T(8,128)S(1)}, f32[8,128]{1,0:T(8,128)S(1)}) custom-call(s32[18]{0:T(128)S(1)} %get-tuple-element.41.plan.refs_0_, bf16[512,512]{1,0:T(8,128)(2,1)S(1)} %get-tuple-element.43.refs_0_.x.refs_2_.refs_3_.refs_4_, bf16[512,512]{1,0:T(8,128)(2,1)S(1)} %get-tuple-element.52.refs_1_.x.refs_4_.refs_5_, ...), custom_call_target="tpu_custom_call" | custom-call | flops 2326440704 | bytes 8738133 | tf_op jit(solution)/shard_map/pallas_call | solution.py:322
  97.4 1.1 collective-permute-done.6.from_far
  98.6 1.8 %shard_map.118 = (f32[512,512]{1,0:T(8,128)S(1)}, f32[32,1,128]{2,1,0:T(1,128)S(1)}) custom-call(s32[18]{0:T(128)S(1)} %get-tuple-element.41.plan.refs_0_, bf16[512,512]{1,0:T(8,128)(2,1)S(1)} %get-tuple-element.43.refs_0_.x.refs_2_.refs_3_.refs_4_, bf16[512,512]{1,0:T(8,128)(2,1)S(1)} %get-tuple-element.52.refs_1_.x.refs_4_.refs_5_, ...), custom_call_target="tpu_custom_call" | custom-call | flops 1048576 | bytes 4196352 | tf_op jit(solution)/shard_map/pallas_call | solution.py:322
  100.4 12.2 %all_to_all.22.refs_1_ = f32[32,1,128]{2,1,0:T(1,128)S(1)} all-to-all(f32[32,1,128]{2,1,0:T(1,128)S(1)} %get-tuple-element.65), channel_id=1, replica_groups=mesh['seg'=4,'sec'=32] {'sec'}, dimensions={0} | all-to-all | bytes 32768 | tf_op jit(solution)/shard_map/all_to_all | solution.py:419
  112.6 7.1 %shard_map.119 = (bf16[512,512]{1,0:T(8,128)(2,1)S(1)}, bf16[512,512]{1,0:T(8,128)(2,1)S(1)}, f32[2,512,512]{2,1,0:T(8,128)S(1)}, f32[8,128]{1,0:T(8,128)S(1)}) custom-call(s32[18]{0:T(128)S(1)} %get-tuple-element.41.plan.refs_0_, f32[32,1,128]{2,1,0:T(1,128)S(1)} %all_to_all.22.refs_1_, f32[8,128]{1,0:T(8,128)S(1)} %get-tuple-element.58.refs_2_.refs_1_, ...), custom_call_target="tpu_custom_call" | custom-call | flops 2326440704 | bytes 8738133 | tf_op jit(solution)/shard_map/pallas_call | solution.py:322
  119.7 2.7 %collective-permute-start.8 = (bf16[512,512]{1,0:T(8,128)(2,1)S(1)}, bf16[512,512]{1,0:T(8,128)(2,1)S(1)}, u32[]{:S(2)}, u32[]{:S(2)}) collective-permute-start(bf16[512,512]{1,0:T(8,128)(2,1)S(1)} %get-tuple-element.70), channel_id=1, source_target_pairs={{1,2},{3,4},{5,6},{7,8},{9,10},{11,12},{13,14},{15,16},{17,18},{19... | collective-permute-start | bytes 1572872 | tf_op jit(solution)/shard_map/ppermute | solution.py:340
  122.5 3.2 %shard_map.122 = bf16[512,512]{1,0:T(8,128)(2,1)S(1)} custom-call(s32[18]{0:T(128)S(1)} %get-tuple-element.41.plan.refs_0_, bf16[512,512]{1,0:T(8,128)(2,1)S(1)} %get-tuple-element.68.refs_3_.x.refs_7_, f32[2,512,512]{2,1,0:T(8,128)S(1)} %get-tuple-element.71.head_sums, bf16[13,512,512]{2,1,0:T(8,128)(2,1)S(1)} %bitcast.23, bf16[13,512,512]{2,1,0:T(8,128)(2,1)S(1)} %bitcast.37), custom_call_target="tpu_custom_call" | custom-call | flops 2326440704 | bytes 8738133 | tf_op jit(solution)/shard_map/pallas_call | solution.py:322
  125.8 3.6 %shard_map.120 = (f32[512,512]{1,0:T(8,128)S(1)}, f32[8,128]{1,0:T(8,128)S(1)}) custom-call(s32[18]{0:T(128)S(1)} %get-tuple-element.41.plan.refs_0_, bf16[512,512]{1,0:T(8,128)(2,1)S(1)} %get-tuple-element.43.refs_0_.x.refs_2_.refs_3_.refs_4_, bf16[512,512]{1,0:T(8,128)(2,1)S(1)} %get-tuple-element.52.refs_1_.x.refs_4_.refs_5_, ...), custom_call_target="tpu_custom_call" | custom-call | flops 2326440704 | bytes 8738133 | tf_op jit(solution)/shard_map/pallas_call | solution.py:322
  129.4 0.8 collective-permute-done.8.from_far
  130.3 2.1 %shard_map.123 = (f32[512,512]{1,0:T(8,128)S(1)}, f32[32,1,128]{2,1,0:T(1,128)S(1)}) custom-call(s32[18]{0:T(128)S(1)} %get-tuple-element.41.plan.refs_0_, bf16[512,512]{1,0:T(8,128)(2,1)S(1)} %get-tuple-element.43.refs_0_.x.refs_2_.refs_3_.refs_4_, bf16[512,512]{1,0:T(8,128)(2,1)S(1)} %get-tuple-element.52.refs_1_.x.refs_4_.refs_5_, ...), custom_call_target="tpu_custom_call" | custom-call | flops 1048576 | bytes 4196352 | tf_op jit(solution)/shard_map/pallas_call | solution.py:322
  132.5 12.2 %all_to_all.23.refs_0_ = f32[32,1,128]{2,1,0:T(1,128)S(1)} all-to-all(f32[32,1,128]{2,1,0:T(1,128)S(1)} %get-tuple-element.73), channel_id=1, replica_groups=mesh['seg'=4,'sec'=32] {'sec'}, dimensions={0} | all-to-all | bytes 32768 | tf_op jit(solution)/shard_map/all_to_all | solution.py:419
  144.6 4.0 %shard_map.124 = (bf16[512,512]{1,0:T(8,128)(2,1)}, f32[512,512]{1,0:T(8,128)}, f32[4,4]{1,0:T(4,128)}) custom-call(f32[32,1,128]{2,1,0:T(1,128)S(1)} %all_to_all.23.refs_0_, f32[8,128]{1,0:T(8,128)S(1)} %get-tuple-element.58.refs_2_.refs_1_, f32[8,128]{1,0:T(8,128)S(1)} %get-tuple-element.66.refs_3_.refs_2_, f32[8,128]{1,0:T(8,128)S(1)} %get-tuple-element.74.refs_3_, ...), custom_call_target="tpu_custom_call" | custom-call | flops 1048576 | bytes 4196352 | tf_op jit(solution)/shard_map/pallas_call | solution.py:322
  (28 shorter events, 2.2 us)
Async XLA Ops:
  0.6 14.3 %collective-permute-start = (bf16[512,512]{1,0:T(8,128)(2,1)}, bf16[512,512]{1,0:T(8,128)(2,1)S(1)}, u32[]{:S(2)}, u32[]{:S(2)}) collective-permute-start(bf16[512,512]{1,0:T(8,128)(2,1)} %bitcast.43), channel_id=1, source_target_pairs={{32,0},{64,32},{96,64},{0,96},{33,1},{65,33},{97,65},{1,97},{34,2}... | collective-permute-start | bytes 1572872 | tf_op jit(solution)/shard_map/ppermute | solution.py:360
  1.2 13.7 %collective-permute-start.1 = (bf16[1,512]{1,0:T(2,128)(2,1)}, bf16[1,512]{1,0:T(2,128)(2,1)S(1)}, u32[]{:S(2)}, u32[]{:S(2)}) collective-permute-start(bf16[1,512]{1,0:T(2,128)(2,1)} %bitcast.45), channel_id=1, source_target_pairs={{32,0},{64,32},{96,64},{0,96},{33,1},{65,33},{97,65},{1,97},{34,2}... | collective-permute-start | bytes 3080 | tf_op jit(solution)/shard_map/ppermute | solution.py:360
  1.5 0.7 copy-start
  2.2 0.7 copy-start.1
  14.9 11.3 %slice-start = ((s8[6815744]{0:T(1024)(128)(4,1)}), s8[4194304]{0:T(1024)(128)(4,1)S(1)}, s32[]{:S(2)}) async-start(s8[6815744]{0:T(1024)(128)(4,1)} %bitcast.12), calls=%async_computation.4 | async-start | bytes 8388608
  14.9 11.3 %slice-start.2 = ((s8[6815744]{0:T(1024)(128)(4,1)}), s8[4194304]{0:T(1024)(128)(4,1)S(1)}, s32[]{:S(2)}) async-start(s8[6815744]{0:T(1024)(128)(4,1)} %bitcast.26), calls=%async_computation.6 | async-start | bytes 8388608
  14.9 11.3 %slice-start.1 = ((s8[6815744]{0:T(1024)(128)(4,1)}), s8[2621440]{0:T(1024)(128)(4,1)S(1)}, s32[]{:S(2)}) async-start(s8[6815744]{0:T(1024)(128)(4,1)} %bitcast.12), calls=%async_computation.5 | async-start | bytes 5242880
  14.9 11.3 %slice-start.3 = ((s8[6815744]{0:T(1024)(128)(4,1)}), s8[2621440]{0:T(1024)(128)(4,1)S(1)}, s32[]{:S(2)}) async-start(s8[6815744]{0:T(1024)(128)(4,1)} %bitcast.26), calls=%async_computation.7 | async-start | bytes 5242880
  21.6 11.5 %collective-permute-start.2 = (bf16[512,512]{1,0:T(8,128)(2,1)S(1)}, bf16[512,512]{1,0:T(8,128)(2,1)S(1)}, u32[]{:S(2)}, u32[]{:S(2)}) collective-permute-start(bf16[512,512]{1,0:T(8,128)(2,1)S(1)} %get-tuple-element.46), channel_id=1, source_target_pairs={{1,2},{3,4},{5,6},{7,8},{9,10},{11,12},{13,14},{15,16},{17,18},{19... | collective-permute-start | bytes 1572872 | tf_op jit(solution)/shard_map/ppermute | solution.py:340
  29.5 3.8 %collective-permute-start.3 = (bf16[512,512]{1,0:T(8,128)(2,1)S(1)}, bf16[512,512]{1,0:T(8,128)(2,1)S(1)}, u32[]{:S(2)}, u32[]{:S(2)}) collective-permute-start(bf16[512,512]{1,0:T(8,128)(2,1)S(1)} %shard_map.107), channel_id=1, source_target_pairs={{0,1},{2,3},{4,5},{6,7},{8,9},{10,11},{12,13},{14,15},{16,17},{18,... | collective-permute-start | bytes 1572872 | tf_op jit(solution)/shard_map/ppermute | solution.py:340
  56.9 10.5 %collective-permute-start.4 = (bf16[512,512]{1,0:T(8,128)(2,1)S(1)}, bf16[512,512]{1,0:T(8,128)(2,1)S(1)}, u32[]{:S(2)}, u32[]{:S(2)}) collective-permute-start(bf16[512,512]{1,0:T(8,128)(2,1)S(1)} %get-tuple-element.54), channel_id=1, source_target_pairs={{1,2},{3,4},{5,6},{7,8},{9,10},{11,12},{13,14},{15,16},{17,18},{19... | collective-permute-start | bytes 1572872 | tf_op jit(solution)/shard_map/ppermute | solution.py:340
  63.0 4.5 %collective-permute-start.5 = (bf16[512,512]{1,0:T(8,128)(2,1)S(1)}, bf16[512,512]{1,0:T(8,128)(2,1)S(1)}, u32[]{:S(2)}, u32[]{:S(2)}) collective-permute-start(bf16[512,512]{1,0:T(8,128)(2,1)S(1)} %shard_map.112), channel_id=1, source_target_pairs={{0,1},{2,3},{4,5},{6,7},{8,9},{10,11},{12,13},{14,15},{16,17},{18,... | collective-permute-start | bytes 1572872 | tf_op jit(solution)/shard_map/ppermute | solution.py:340
  88.0 10.5 %collective-permute-start.6 = (bf16[512,512]{1,0:T(8,128)(2,1)S(1)}, bf16[512,512]{1,0:T(8,128)(2,1)S(1)}, u32[]{:S(2)}, u32[]{:S(2)}) collective-permute-start(bf16[512,512]{1,0:T(8,128)(2,1)S(1)} %get-tuple-element.62), channel_id=1, source_target_pairs={{1,2},{3,4},{5,6},{7,8},{9,10},{11,12},{13,14},{15,16},{17,18},{19... | collective-permute-start | bytes 1572872 | tf_op jit(solution)/shard_map/ppermute | solution.py:340
  93.9 4.7 %collective-permute-start.7 = (bf16[512,512]{1,0:T(8,128)(2,1)S(1)}, bf16[512,512]{1,0:T(8,128)(2,1)S(1)}, u32[]{:S(2)}, u32[]{:S(2)}) collective-permute-start(bf16[512,512]{1,0:T(8,128)(2,1)S(1)} %shard_map.117), channel_id=1, source_target_pairs={{0,1},{2,3},{4,5},{6,7},{8,9},{10,11},{12,13},{14,15},{16,17},{18,... | collective-permute-start | bytes 1572872 | tf_op jit(solution)/shard_map/ppermute | solution.py:340
  119.7 10.5 %collective-permute-start.8 = (bf16[512,512]{1,0:T(8,128)(2,1)S(1)}, bf16[512,512]{1,0:T(8,128)(2,1)S(1)}, u32[]{:S(2)}, u32[]{:S(2)}) collective-permute-start(bf16[512,512]{1,0:T(8,128)(2,1)S(1)} %get-tuple-element.70), channel_id=1, source_target_pairs={{1,2},{3,4},{5,6},{7,8},{9,10},{11,12},{13,14},{15,16},{17,18},{19... | collective-permute-start | bytes 1572872 | tf_op jit(solution)/shard_map/ppermute | solution.py:340
  125.7 4.7 %collective-permute-start.9 = (bf16[512,512]{1,0:T(8,128)(2,1)S(1)}, bf16[512,512]{1,0:T(8,128)(2,1)S(1)}, u32[]{:S(2)}, u32[]{:S(2)}) collective-permute-start(bf16[512,512]{1,0:T(8,128)(2,1)S(1)} %shard_map.122), channel_id=1, source_target_pairs={{0,1},{2,3},{4,5},{6,7},{8,9},{10,11},{12,13},{14,15},{16,17},{18,... | collective-permute-start | bytes 1572872 | tf_op jit(solution)/shard_map/ppermute | solution.py:340
